TPU v7x, 256 devices: a whole 4x4x8 slice. The times are simulated.
256 devices in a mesh: day: 8 (over y, z_lo), sta: 32 (over z_hi, x, core).
Axes of the slice: x: 4, y: 4, z: 8 (z_hi: 4, z_lo: 2; z = z_hi * 2 + z_lo), core: 2. Of those that a mesh axis runs over, the one named last changes fastest.
Arguments:
- spectra: bfloat16 [8, 512, 8, 2, 3584], P('day', 'sta'), may hold values from -1600 to 1600, as said below
- hour_flags: int32 [8, 512, 8], P('day', 'sta'), may hold values 0 or 1
- sources: int32 [2, 8], replicated, may hold values from 0 to 511
- station_rows: int32 [512], replicated, may hold values from 0 to 511, each once
Outputs:
- stacked: float32 [16, 512, 1024], P(None, 'sta', 'day')
Inputs may be any that keep to these rules, and one draw needn't show every extreme that they name: `spectra`: spectral values.
All inputs are finite; a program needn't handle non-finite values. No bound on the sum of `hour_flags` on one device may be relied on, other than what follows from the above.
Results may differ from a plain program's by a relative error of at most 0.0034.
Values may be sent and summed in bfloat16 or wider, within the bound.
A program may use at most 128 MiB of HBM per device.

v0:
```python
import math

import jax
import jax.numpy as jnp
from jax import lax
from jax.sharding import PartitionSpec as P

BINS = 3584
LAGS = 1024


EPSILON = 1e-06


def broadcast(value, axis, source):
    kept = jnp.where(lax.axis_index(axis) == source, value, 0).astype(value.dtype)
    return lax.psum(kept, axis)


def to_lags(cosine_sum, sine_sum, first_bin):
    bin_count = cosine_sum.shape[-1]
    leading = cosine_sum.shape[0] * cosine_sum.shape[1]
    cosine_rows = cosine_sum.reshape(leading, bin_count)
    sine_rows = sine_sum.reshape(leading, bin_count)
    block_bins = math.gcd(bin_count, 512)
    lag_values = jnp.arange(LAGS, dtype=jnp.int32) - LAGS // 2

    def add_block(counter, running):
        offset = counter * block_bins
        bins_now = first_bin + offset + jnp.arange(block_bins, dtype=jnp.int32)
        phases = jnp.mod(bins_now[:, None] * lag_values[None, :], 2 * BINS)
        angles = phases.astype(jnp.float32) * (math.pi / BINS)
        cosine_part = lax.dynamic_slice_in_dim(cosine_rows, offset, block_bins, 1)
        sine_part = lax.dynamic_slice_in_dim(sine_rows, offset, block_bins, 1)
        running = running + jnp.dot(cosine_part, jnp.cos(angles), precision=lax.Precision.HIGHEST)
        return running - jnp.dot(sine_part, jnp.sin(angles), precision=lax.Precision.HIGHEST)

    running = lax.fori_loop(
        0, bin_count // block_bins, add_block, jnp.zeros((leading, LAGS), jnp.float32)
    )
    running = running / math.sqrt(BINS)
    return running.reshape(cosine_sum.shape[0], cosine_sum.shape[1], LAGS)


def shards(spectra, hour_flags, sources, station_rows):
    receivers = spectra.shape[1]
    values = spectra[0].astype(jnp.float32)
    power_mean = jnp.mean(values * values, axis=(2, 3))
    valid = hour_flags[0].astype(jnp.float32)
    whitened = (values * (valid / jnp.sqrt(power_mean + EPSILON))[:, :, None, None]).astype(
        jnp.bfloat16
    )
    results = []
    for round_index in range(sources.shape[0]):
        source_rows = station_rows[sources[round_index]]
        spec_pieces = []
        flag_pieces = []
        for source_index in range(source_rows.shape[0]):
            target = source_rows[source_index]
            owner = target // receivers
            offset = target - owner * receivers
            own_spec = lax.dynamic_index_in_dim(whitened, offset, 0, keepdims=False)
            own_flags = lax.dynamic_index_in_dim(valid, offset, 0, keepdims=False).astype(
                jnp.bfloat16
            )
            got_spec, got_flags = (
                broadcast(own_spec, "sta", owner),
                broadcast(own_flags, "sta", owner),
            )
            spec_pieces.append(got_spec)
            flag_pieces.append(got_flags)
        source_spec = jnp.stack(spec_pieces)
        source_valid = jnp.stack(flag_pieces).astype(jnp.float32)
        source_wide = source_spec.astype(jnp.float32)[:, None]
        receiver_wide = whitened.astype(jnp.float32)[None]
        cosine_sum = jnp.sum(
            source_wide[:, :, :, 0] * receiver_wide[:, :, :, 0]
            + source_wide[:, :, :, 1] * receiver_wide[:, :, :, 1],
            axis=2,
        )
        sine_sum = jnp.sum(
            source_wide[:, :, :, 1] * receiver_wide[:, :, :, 0]
            - source_wide[:, :, :, 0] * receiver_wide[:, :, :, 1],
            axis=2,
        )
        intersection = jnp.dot(source_valid, valid.T, precision=lax.Precision.HIGHEST)
        weights = (1.0 / jnp.maximum(intersection, 1.0))[:, :, None]
        cosine_sum = cosine_sum * weights
        sine_sum = sine_sum * weights
        term = to_lags(cosine_sum, sine_sum, 0)
        stacked = lax.psum_scatter(term, "day", scatter_dimension=2, tiled=True)
        results.append(stacked)
    return jnp.concatenate(results, axis=0)


def solution(mesh):
    in_specs = (P("day", "sta", None, None, None), P("day", "sta", None), P(), P())
    out_specs = P(None, "sta", "day")
    return jax.shard_map(shards, mesh=mesh, in_specs=in_specs, out_specs=out_specs, check_vma=False)
```

profile of v0, /device:TPU:1, one launch (start us, length us, event | category | flops | bytes accessed | tf_op | source)
XLA Modules:
  0.0 771.8 jit_solution(15948929472927270565)
XLA Ops:
  61.1 2.0 fusion.76
  63.0 1.6 fusion.77
  64.6 1.6 fusion.97
  66.2 2.0 fusion.91
  68.2 2.3 fusion.82
  71.1 74.6 %all-reduce = (bf16[1,8]{1,0:T(2,128)(2,1)S(1)}, bf16[1,8]{1,0:T(2,128)(2,1)S(1)}, bf16[1,8]{1,0:T(2,128)(2,1)S(1)}, bf16[1,8]{1,0:T(2,128)(2,1)S(1)}, bf16[1,8]...) all-reduce(bf16[1,8]{1,0:T(2,128)(2,1)S(1)} %bitcast.185, ...), channel_id=1, replica_groups=mesh['day'=8,'sta'=32] {'sta'}, use_global_device_ids=true, to_apply=%region_31.32 | all-reduce | flops 128 | bytes 512 | tf_op jit(solution)/shard_map/psum | solution.py:17
  146.8 1.5 slice_bitcast_fusion.1
  148.3 219.6 %all-reduce.4.cloned.1.call-done = (bf16[1,1,8,2,3584]{4,2,3,1,0:T(8,128)(2,1)}, bf16[1,1,8,2,3584]{4,2,3,1,0:T(8,128)(2,1)}, bf16[1,1,8,2,3584]{4,2,3,1,0:T(8,1...) async-done(((bf16[1,1,8,2,3584]{4,2,3,1,0:T(8,128)(2,1)}, ...) | async-done | bytes 1835024 | tf_op jit(solution)/shard_map/psum | solution.py:17
  368.8 0.9 constant_dynamic-update-slice_fusion.14
  369.7 0.9 constant_dynamic-update-slice_fusion.13
  373.4 0.9 constant_dynamic-update-slice_fusion.9
  374.3 0.9 constant_dynamic-update-slice_fusion.8
  377.0 1.4 copy-done.2
  378.3 24.6 %subtract_reduce_fusion.1 = (f32[8,16,3584]{2,1,0:T(8,128)S(1)}, f32[8,16,3584]{2,1,0:T(8,128)S(1)}, f32[8,16,3584]{2,1,0:T(8,128)}, f32[8,16,3584]{2,1,0:T(8,128)}) fusion(f32[16,8,3584]{2,1,0:T(8,128)S(1)} %copy-done.2, f32[8,8,3584]{2,1,0:T(8,128)S(1)} %get-tuple-element.382, f32[16,8,3584]{2,1,0:T(8,128)S(1)} %get-tuple-element.377, ...), kind=kLoop, calls=%fused_computation.68 | loop fusion | flops 56885248 | bytes 14680064 | tf_op jit(solution)/shard_map/reduce_sum | solution.py:81
  403.0 2.3 bitcast_multiply_fusion.2
  405.2 158.9 %while.32 = (s32[]{:T(128)}, f32[128,1024]{1,0:T(8,128)S(1)}, f32[128,3584]{1,0:T(8,128)}, f32[128,3584]{1,0:T(8,128)}, s32[]{:T(128)}, /*index=5*/s32[]{:T(128)}, s32[]{:T(128)}, s32[]{:T(128)}) while((s32[]{:T(128)}, f32[128,1024]{1,0:T(8,128)S(1)}, f32[128,3584]{1,0:T(8,128)}, f32[128,3584]{1,0:T(8,128)}, s32[]{:T(128)}, ...), condition=%wide.region_20.21_spmd.clone, body=%wide.region_19.20_spmd.clone.sunk | while | flops 1620444672 | bytes 2640025 | solution.py:38
  418.9 10.3 %fusion.173 = f32[128,1024]{1,0:T(8,128)S(1)} fusion(s32[1024]{0:T(1024)S(1)} %iota_add_fusion.8, s32[512]{0:T(512)S(1)} %iota_add_fusion.9, f32[128,3584]{1,0:T(8,128)} %get-tuple-element.517, s32[]{:T(128)S(6)} %select_n.808), kind=kOutput, calls=%fused_computation.7.clone.1 | convolution fusion | flops 810024960 | bytes 792580 | tf_op jit(solution)/shard_map/while/body/eval_jaxpr/dot_general | solution.py:36
  429.2 10.4 %fusion.174 = f32[128,1024]{1,0:T(8,128)S(1)} fusion(f32[128,1024]{1,0:T(8,128)S(1)} %fusion.173, s32[1024]{0:T(1024)S(1)} %iota_add_fusion.8, s32[512]{0:T(512)S(1)} %iota_add_fusion.9, f32[128,1024]{1,0:T(8,128)S(1)} %get-tuple-element.507, f32[128,3584]{1,0:T(8,128)} %get-tuple-element.516, s32[]{:T(128)S(6)} %select_n.808, pred[]{:T(512)S(6)} %compare.38), kind=kOutput, calls=%fused_computation.16.clone.1 | convolution fusion | flops 810418176 | bytes 1841157 | tf_op jit(solution)/shard_map/while/body/eval_jaxpr/dot_general | solution.py:35
  439.6 10.3 %fusion.173 = f32[128,1024]{1,0:T(8,128)S(1)} fusion(s32[1024]{0:T(1024)S(1)} %iota_add_fusion.8, s32[512]{0:T(512)S(1)} %iota_add_fusion.9, f32[128,3584]{1,0:T(8,128)} %get-tuple-element.517, s32[]{:T(128)S(6)} %select_n.808), kind=kOutput, calls=%fused_computation.7.clone.1 | convolution fusion | flops 810024960 | bytes 792580 | tf_op jit(solution)/shard_map/while/body/eval_jaxpr/dot_general | solution.py:36
  450.0 10.4 %fusion.174 = f32[128,1024]{1,0:T(8,128)S(1)} fusion(f32[128,1024]{1,0:T(8,128)S(1)} %fusion.173, s32[1024]{0:T(1024)S(1)} %iota_add_fusion.8, s32[512]{0:T(512)S(1)} %iota_add_fusion.9, f32[128,1024]{1,0:T(8,128)S(1)} %get-tuple-element.507, f32[128,3584]{1,0:T(8,128)} %get-tuple-element.516, s32[]{:T(128)S(6)} %select_n.808, pred[]{:T(512)S(6)} %compare.38), kind=kOutput, calls=%fused_computation.16.clone.1 | convolution fusion | flops 810418176 | bytes 1841157 | tf_op jit(solution)/shard_map/while/body/eval_jaxpr/dot_general | solution.py:35
  460.4 10.3 %fusion.173 = f32[128,1024]{1,0:T(8,128)S(1)} fusion(s32[1024]{0:T(1024)S(1)} %iota_add_fusion.8, s32[512]{0:T(512)S(1)} %iota_add_fusion.9, f32[128,3584]{1,0:T(8,128)} %get-tuple-element.517, s32[]{:T(128)S(6)} %select_n.808), kind=kOutput, calls=%fused_computation.7.clone.1 | convolution fusion | flops 810024960 | bytes 792580 | tf_op jit(solution)/shard_map/while/body/eval_jaxpr/dot_general | solution.py:36
  470.7 10.3 %fusion.174 = f32[128,1024]{1,0:T(8,128)S(1)} fusion(f32[128,1024]{1,0:T(8,128)S(1)} %fusion.173, s32[1024]{0:T(1024)S(1)} %iota_add_fusion.8, s32[512]{0:T(512)S(1)} %iota_add_fusion.9, f32[128,1024]{1,0:T(8,128)S(1)} %get-tuple-element.507, f32[128,3584]{1,0:T(8,128)} %get-tuple-element.516, s32[]{:T(128)S(6)} %select_n.808, pred[]{:T(512)S(6)} %compare.38), kind=kOutput, calls=%fused_computation.16.clone.1 | convolution fusion | flops 810418176 | bytes 1841157 | tf_op jit(solution)/shard_map/while/body/eval_jaxpr/dot_general | solution.py:35
  481.1 10.3 %fusion.173 = f32[128,1024]{1,0:T(8,128)S(1)} fusion(s32[1024]{0:T(1024)S(1)} %iota_add_fusion.8, s32[512]{0:T(512)S(1)} %iota_add_fusion.9, f32[128,3584]{1,0:T(8,128)} %get-tuple-element.517, s32[]{:T(128)S(6)} %select_n.808), kind=kOutput, calls=%fused_computation.7.clone.1 | convolution fusion | flops 810024960 | bytes 792580 | tf_op jit(solution)/shard_map/while/body/eval_jaxpr/dot_general | solution.py:36
  491.5 10.3 %fusion.174 = f32[128,1024]{1,0:T(8,128)S(1)} fusion(f32[128,1024]{1,0:T(8,128)S(1)} %fusion.173, s32[1024]{0:T(1024)S(1)} %iota_add_fusion.8, s32[512]{0:T(512)S(1)} %iota_add_fusion.9, f32[128,1024]{1,0:T(8,128)S(1)} %get-tuple-element.507, f32[128,3584]{1,0:T(8,128)} %get-tuple-element.516, s32[]{:T(128)S(6)} %select_n.808, pred[]{:T(512)S(6)} %compare.38), kind=kOutput, calls=%fused_computation.16.clone.1 | convolution fusion | flops 810418176 | bytes 1841157 | tf_op jit(solution)/shard_map/while/body/eval_jaxpr/dot_general | solution.py:35
  501.9 10.3 %fusion.173 = f32[128,1024]{1,0:T(8,128)S(1)} fusion(s32[1024]{0:T(1024)S(1)} %iota_add_fusion.8, s32[512]{0:T(512)S(1)} %iota_add_fusion.9, f32[128,3584]{1,0:T(8,128)} %get-tuple-element.517, s32[]{:T(128)S(6)} %select_n.808), kind=kOutput, calls=%fused_computation.7.clone.1 | convolution fusion | flops 810024960 | bytes 792580 | tf_op jit(solution)/shard_map/while/body/eval_jaxpr/dot_general | solution.py:36
  512.2 10.3 %fusion.174 = f32[128,1024]{1,0:T(8,128)S(1)} fusion(f32[128,1024]{1,0:T(8,128)S(1)} %fusion.173, s32[1024]{0:T(1024)S(1)} %iota_add_fusion.8, s32[512]{0:T(512)S(1)} %iota_add_fusion.9, f32[128,1024]{1,0:T(8,128)S(1)} %get-tuple-element.507, f32[128,3584]{1,0:T(8,128)} %get-tuple-element.516, s32[]{:T(128)S(6)} %select_n.808, pred[]{:T(512)S(6)} %compare.38), kind=kOutput, calls=%fused_computation.16.clone.1 | convolution fusion | flops 810418176 | bytes 1841157 | tf_op jit(solution)/shard_map/while/body/eval_jaxpr/dot_general | solution.py:35
  522.6 10.3 %fusion.173 = f32[128,1024]{1,0:T(8,128)S(1)} fusion(s32[1024]{0:T(1024)S(1)} %iota_add_fusion.8, s32[512]{0:T(512)S(1)} %iota_add_fusion.9, f32[128,3584]{1,0:T(8,128)} %get-tuple-element.517, s32[]{:T(128)S(6)} %select_n.808), kind=kOutput, calls=%fused_computation.7.clone.1 | convolution fusion | flops 810024960 | bytes 792580 | tf_op jit(solution)/shard_map/while/body/eval_jaxpr/dot_general | solution.py:36
  533.0 10.3 %fusion.174 = f32[128,1024]{1,0:T(8,128)S(1)} fusion(f32[128,1024]{1,0:T(8,128)S(1)} %fusion.173, s32[1024]{0:T(1024)S(1)} %iota_add_fusion.8, s32[512]{0:T(512)S(1)} %iota_add_fusion.9, f32[128,1024]{1,0:T(8,128)S(1)} %get-tuple-element.507, f32[128,3584]{1,0:T(8,128)} %get-tuple-element.516, s32[]{:T(128)S(6)} %select_n.808, pred[]{:T(512)S(6)} %compare.38), kind=kOutput, calls=%fused_computation.16.clone.1 | convolution fusion | flops 810418176 | bytes 1841157 | tf_op jit(solution)/shard_map/while/body/eval_jaxpr/dot_general | solution.py:35
  543.4 10.3 %fusion.173 = f32[128,1024]{1,0:T(8,128)S(1)} fusion(s32[1024]{0:T(1024)S(1)} %iota_add_fusion.8, s32[512]{0:T(512)S(1)} %iota_add_fusion.9, f32[128,3584]{1,0:T(8,128)} %get-tuple-element.517, s32[]{:T(128)S(6)} %select_n.808), kind=kOutput, calls=%fused_computation.7.clone.1 | convolution fusion | flops 810024960 | bytes 792580 | tf_op jit(solution)/shard_map/while/body/eval_jaxpr/dot_general | solution.py:36
  553.7 10.3 %fusion.174 = f32[128,1024]{1,0:T(8,128)S(1)} fusion(f32[128,1024]{1,0:T(8,128)S(1)} %fusion.173, s32[1024]{0:T(1024)S(1)} %iota_add_fusion.8, s32[512]{0:T(512)S(1)} %iota_add_fusion.9, f32[128,1024]{1,0:T(8,128)S(1)} %get-tuple-element.507, f32[128,3584]{1,0:T(8,128)} %get-tuple-element.516, s32[]{:T(128)S(6)} %select_n.808, pred[]{:T(512)S(6)} %compare.38), kind=kOutput, calls=%fused_computation.16.clone.1 | convolution fusion | flops 810418176 | bytes 1841157 | tf_op jit(solution)/shard_map/while/body/eval_jaxpr/dot_general | solution.py:35
  565.1 3.8 bitcast_multiply_fusion
  568.9 158.7 %while.33 = (s32[]{:T(128)}, f32[128,1024]{1,0:T(8,128)S(1)}, f32[128,3584]{1,0:T(8,128)}, f32[128,3584]{1,0:T(8,128)}, s32[]{:T(128)}, /*index=5*/s32[]{:T(128)}, s32[]{:T(128)}, s32[]{:T(128)}) while((s32[]{:T(128)}, f32[128,1024]{1,0:T(8,128)S(1)}, f32[128,3584]{1,0:T(8,128)}, f32[128,3584]{1,0:T(8,128)}, s32[]{:T(128)}, ...), condition=%wide.region_41.42_spmd.clone, body=%wide.region_40.41_spmd.clone.sunk | while | flops 1620444672 | bytes 2640025 | solution.py:38
  582.2 10.4 %fusion.179 = f32[128,1024]{1,0:T(8,128)S(1)} fusion(s32[1024]{0:T(1024)S(1)} %iota_add_fusion.10, s32[512]{0:T(512)S(1)} %iota_add_fusion.11, f32[128,3584]{1,0:T(8,128)} %get-tuple-element.493, s32[]{:T(128)S(6)} %select_n.811), kind=kOutput, calls=%fused_computation.38.clone.1 | convolution fusion | flops 810024960 | bytes 792580 | tf_op jit(solution)/shard_map/while/body/eval_jaxpr/dot_general | solution.py:36
  592.6 10.3 %fusion.180 = f32[128,1024]{1,0:T(8,128)S(1)} fusion(f32[128,1024]{1,0:T(8,128)S(1)} %fusion.179, s32[1024]{0:T(1024)S(1)} %iota_add_fusion.10, s32[512]{0:T(512)S(1)} %iota_add_fusion.11, f32[128,1024]{1,0:T(8,128)S(1)} %get-tuple-element.483, f32[128,3584]{1,0:T(8,128)} %get-tuple-element.492, s32[]{:T(128)S(6)} %select_n.811, pred[]{:T(512)S(6)} %compare.39), kind=kOutput, calls=%fused_computation.47.clone.1 | convolution fusion | flops 810418176 | bytes 1841157 | tf_op jit(solution)/shard_map/while/body/eval_jaxpr/dot_general | solution.py:35
  603.0 10.3 %fusion.179 = f32[128,1024]{1,0:T(8,128)S(1)} fusion(s32[1024]{0:T(1024)S(1)} %iota_add_fusion.10, s32[512]{0:T(512)S(1)} %iota_add_fusion.11, f32[128,3584]{1,0:T(8,128)} %get-tuple-element.493, s32[]{:T(128)S(6)} %select_n.811), kind=kOutput, calls=%fused_computation.38.clone.1 | convolution fusion | flops 810024960 | bytes 792580 | tf_op jit(solution)/shard_map/while/body/eval_jaxpr/dot_general | solution.py:36
  613.4 10.4 %fusion.180 = f32[128,1024]{1,0:T(8,128)S(1)} fusion(f32[128,1024]{1,0:T(8,128)S(1)} %fusion.179, s32[1024]{0:T(1024)S(1)} %iota_add_fusion.10, s32[512]{0:T(512)S(1)} %iota_add_fusion.11, f32[128,1024]{1,0:T(8,128)S(1)} %get-tuple-element.483, f32[128,3584]{1,0:T(8,128)} %get-tuple-element.492, s32[]{:T(128)S(6)} %select_n.811, pred[]{:T(512)S(6)} %compare.39), kind=kOutput, calls=%fused_computation.47.clone.1 | convolution fusion | flops 810418176 | bytes 1841157 | tf_op jit(solution)/shard_map/while/body/eval_jaxpr/dot_general | solution.py:35
  623.8 10.3 %fusion.179 = f32[128,1024]{1,0:T(8,128)S(1)} fusion(s32[1024]{0:T(1024)S(1)} %iota_add_fusion.10, s32[512]{0:T(512)S(1)} %iota_add_fusion.11, f32[128,3584]{1,0:T(8,128)} %get-tuple-element.493, s32[]{:T(128)S(6)} %select_n.811), kind=kOutput, calls=%fused_computation.38.clone.1 | convolution fusion | flops 810024960 | bytes 792580 | tf_op jit(solution)/shard_map/while/body/eval_jaxpr/dot_general | solution.py:36
  634.1 10.3 %fusion.180 = f32[128,1024]{1,0:T(8,128)S(1)} fusion(f32[128,1024]{1,0:T(8,128)S(1)} %fusion.179, s32[1024]{0:T(1024)S(1)} %iota_add_fusion.10, s32[512]{0:T(512)S(1)} %iota_add_fusion.11, f32[128,1024]{1,0:T(8,128)S(1)} %get-tuple-element.483, f32[128,3584]{1,0:T(8,128)} %get-tuple-element.492, s32[]{:T(128)S(6)} %select_n.811, pred[]{:T(512)S(6)} %compare.39), kind=kOutput, calls=%fused_computation.47.clone.1 | convolution fusion | flops 810418176 | bytes 1841157 | tf_op jit(solution)/shard_map/while/body/eval_jaxpr/dot_general | solution.py:35
  644.5 10.3 %fusion.179 = f32[128,1024]{1,0:T(8,128)S(1)} fusion(s32[1024]{0:T(1024)S(1)} %iota_add_fusion.10, s32[512]{0:T(512)S(1)} %iota_add_fusion.11, f32[128,3584]{1,0:T(8,128)} %get-tuple-element.493, s32[]{:T(128)S(6)} %select_n.811), kind=kOutput, calls=%fused_computation.38.clone.1 | convolution fusion | flops 810024960 | bytes 792580 | tf_op jit(solution)/shard_map/while/body/eval_jaxpr/dot_general | solution.py:36
  654.9 10.3 %fusion.180 = f32[128,1024]{1,0:T(8,128)S(1)} fusion(f32[128,1024]{1,0:T(8,128)S(1)} %fusion.179, s32[1024]{0:T(1024)S(1)} %iota_add_fusion.10, s32[512]{0:T(512)S(1)} %iota_add_fusion.11, f32[128,1024]{1,0:T(8,128)S(1)} %get-tuple-element.483, f32[128,3584]{1,0:T(8,128)} %get-tuple-element.492, s32[]{:T(128)S(6)} %select_n.811, pred[]{:T(512)S(6)} %compare.39), kind=kOutput, calls=%fused_computation.47.clone.1 | convolution fusion | flops 810418176 | bytes 1841157 | tf_op jit(solution)/shard_map/while/body/eval_jaxpr/dot_general | solution.py:35
  665.3 10.3 %fusion.179 = f32[128,1024]{1,0:T(8,128)S(1)} fusion(s32[1024]{0:T(1024)S(1)} %iota_add_fusion.10, s32[512]{0:T(512)S(1)} %iota_add_fusion.11, f32[128,3584]{1,0:T(8,128)} %get-tuple-element.493, s32[]{:T(128)S(6)} %select_n.811), kind=kOutput, calls=%fused_computation.38.clone.1 | convolution fusion | flops 810024960 | bytes 792580 | tf_op jit(solution)/shard_map/while/body/eval_jaxpr/dot_general | solution.py:36
  675.6 10.4 %fusion.180 = f32[128,1024]{1,0:T(8,128)S(1)} fusion(f32[128,1024]{1,0:T(8,128)S(1)} %fusion.179, s32[1024]{0:T(1024)S(1)} %iota_add_fusion.10, s32[512]{0:T(512)S(1)} %iota_add_fusion.11, f32[128,1024]{1,0:T(8,128)S(1)} %get-tuple-element.483, f32[128,3584]{1,0:T(8,128)} %get-tuple-element.492, s32[]{:T(128)S(6)} %select_n.811, pred[]{:T(512)S(6)} %compare.39), kind=kOutput, calls=%fused_computation.47.clone.1 | convolution fusion | flops 810418176 | bytes 1841157 | tf_op jit(solution)/shard_map/while/body/eval_jaxpr/dot_general | solution.py:35
  686.0 10.3 %fusion.179 = f32[128,1024]{1,0:T(8,128)S(1)} fusion(s32[1024]{0:T(1024)S(1)} %iota_add_fusion.10, s32[512]{0:T(512)S(1)} %iota_add_fusion.11, f32[128,3584]{1,0:T(8,128)} %get-tuple-element.493, s32[]{:T(128)S(6)} %select_n.811), kind=kOutput, calls=%fused_computation.38.clone.1 | convolution fusion | flops 810024960 | bytes 792580 | tf_op jit(solution)/shard_map/while/body/eval_jaxpr/dot_general | solution.py:36
  696.4 10.3 %fusion.180 = f32[128,1024]{1,0:T(8,128)S(1)} fusion(f32[128,1024]{1,0:T(8,128)S(1)} %fusion.179, s32[1024]{0:T(1024)S(1)} %iota_add_fusion.10, s32[512]{0:T(512)S(1)} %iota_add_fusion.11, f32[128,1024]{1,0:T(8,128)S(1)} %get-tuple-element.483, f32[128,3584]{1,0:T(8,128)} %get-tuple-element.492, s32[]{:T(128)S(6)} %select_n.811, pred[]{:T(512)S(6)} %compare.39), kind=kOutput, calls=%fused_computation.47.clone.1 | convolution fusion | flops 810418176 | bytes 1841157 | tf_op jit(solution)/shard_map/while/body/eval_jaxpr/dot_general | solution.py:35
  706.8 10.3 %fusion.179 = f32[128,1024]{1,0:T(8,128)S(1)} fusion(s32[1024]{0:T(1024)S(1)} %iota_add_fusion.10, s32[512]{0:T(512)S(1)} %iota_add_fusion.11, f32[128,3584]{1,0:T(8,128)} %get-tuple-element.493, s32[]{:T(128)S(6)} %select_n.811), kind=kOutput, calls=%fused_computation.38.clone.1 | convolution fusion | flops 810024960 | bytes 792580 | tf_op jit(solution)/shard_map/while/body/eval_jaxpr/dot_general | solution.py:36
  717.2 10.3 %fusion.180 = f32[128,1024]{1,0:T(8,128)S(1)} fusion(f32[128,1024]{1,0:T(8,128)S(1)} %fusion.179, s32[1024]{0:T(1024)S(1)} %iota_add_fusion.10, s32[512]{0:T(512)S(1)} %iota_add_fusion.11, f32[128,1024]{1,0:T(8,128)S(1)} %get-tuple-element.483, f32[128,3584]{1,0:T(8,128)} %get-tuple-element.492, s32[]{:T(128)S(6)} %select_n.811, pred[]{:T(512)S(6)} %compare.39), kind=kOutput, calls=%fused_computation.47.clone.1 | convolution fusion | flops 810418176 | bytes 1841157 | tf_op jit(solution)/shard_map/while/body/eval_jaxpr/dot_general | solution.py:35
  728.4 35.1 %reduce-scatter.5.cloned.1.call-done = f32[8,16,128]{2,1,0:T(8,128)} async-done(((f32[8,16,1024]{2,1,0:T(8,128)}), f32[8,16,128]{2,1,0:T(8,128)}) %reduce-scatter.5.cloned.1.call-update) | async-done | bytes 65552 | tf_op jit(solution)/shard_map/reduce_scatter | solution.py:91
  763.5 1.5 pad_maximum_fusion
  (98 shorter events, 13.2 us)
Async XLA Ops:
  6.5 0.9 copy-start
  6.5 56.5 %copy-start.1 = (bf16[1,16,8,2,3584]{4,3,2,1,0:T(2,128)(2,1)S(1)}, bf16[1,16,8,2,3584]{4,3,2,1,0:T(2,128)(2,1)}, u32[]{:S(2)}) copy-start(bf16[1,16,8,2,3584]{4,3,2,1,0:T(2,128)(2,1)} %param.8) | copy-start | bytes 5505028
  6.5 361.4 %all-reduce.4.cloned.1.call-start = ((), (), s32[]{:S(2)}) async-start(), calls=%async_computation.4 | async-start | bytes 3670016 | tf_op jit(solution)/shard_map/psum | solution.py:17
  68.2 77.5 %copy-start.12 = (s32[1,16,8]{1,2,0:T(8,128)S(1)}, s32[1,16,8]{1,2,0:T(8,128)}, u32[]{:S(2)}) copy-start(s32[1,16,8]{1,2,0:T(8,128)} %param.9) | copy-start | bytes 1540
  70.5 657.9 %reduce-scatter.3.cloned.1.call-start = ((), (), s32[]{:S(2)}) async-start(), calls=%async_computation.2 | async-start | bytes 589824 | tf_op jit(solution)/shard_map/reduce_scatter | solution.py:91
  375.4 0.9 copy-start.11
  375.4 0.9 copy-start.10
  375.4 1.0 copy-start.9
  375.4 1.0 copy-start.8
  375.4 1.1 copy-start.7
  375.4 1.1 copy-start.6
  375.4 1.2 copy-start.5
  375.4 1.2 copy-start.4
  376.8 1.5 copy-start.2
  405.2 159.8 %copy-start.3 = (f32[8,16,3584]{2,1,0:T(8,128)S(1)}, f32[8,16,3584]{2,1,0:T(8,128)}, u32[]{:S(2)}) copy-start(f32[8,16,3584]{2,1,0:T(8,128)} %get-tuple-element.311) | copy-start | bytes 5505028
  565.0 198.5 %reduce-scatter.5.cloned.1.call-start = ((), (), s32[]{:S(2)}) async-start(), calls=%async_computation.3 | async-start | bytes 589824 | tf_op jit(solution)/shard_map/reduce_scatter | solution.py:91
Sparse Core Ops, SparseCore 0:
  70.7 297.2 all-reduce.3
  565.1 34.9 reduce-scatter.2
  728.5 34.9 reduce-scatter.4
where the time goes:
time: 786 us; the launch traced here: 772 us
  matrix products  290 us (37%)
  waiting for transfers between devices  255 us (32%)
  blocking collectives  74.6 us (9%)
  between operations  63.7 us (8%)
  other arithmetic  46.5 us (6%)
  loops' own time  27.7 us (4%)
  local copies, waits for them, and re-layouts  14.4 us (2%)
    psum x1, waiting for transfers between devices, broadcast(): return lax.psum(kept, axis)  220 us
    dot_general x14, matrix products, add_block(): jnp.dot(cosine_part, jnp.cos(angles), precision=lax.Precision.HIGHEST)  145 us
    dot_general x14, matrix products, add_block(): jnp.dot(sine_part, jnp.sin(angles), precision=lax.Precision.HIGHEST)  145 us
    psum x1, blocking collectives, broadcast(): return lax.psum(kept, axis)  74.6 us
    reduce_scatter x2, waiting for transfers between devices, shards(): stacked = lax.psum_scatter(term, 'day', scatter_dimension=2, tiled=True)  35.1 us
    another operation x2, loops' own time, to_lags(): lax.fori_loop(0, bin_count // block_bins, add_block, jnp.zeros((leading,...  27.7 us
    reduce_sum x1, other arithmetic, shards(): jnp.sum(source_wide[:, :, :, 1] * receiver_wide[:, :, :, 0] - source_wide...  24.6 us
  transfers between devices with their start and end apart: 3, of which 2 were waited for; matrix products, arithmetic and copies ran while one was open for 20% of the time, Pallas kernels for 0%

commit v1 on v0

v1 whole, which is shorter than its diff:
```python
import functools
import math

import jax
import jax.numpy as jnp
import ml_dtypes
import numpy as np
from jax import lax
from jax.experimental import pallas as pl
from jax.experimental.pallas import tpu as pltpu
from jax.sharding import PartitionSpec as P

BINS = 3584
LAGS = 1024
HALF = LAGS // 2
QUARTER = BINS // 4
EPSILON = 1e-06
SLOTS = 4
MESH = pl.DeviceIdType.MESH
BF16 = jnp.bfloat16
F32 = jnp.float32


def tables():
    bins = np.arange(BINS, dtype=np.int64)[:, None]
    half_lags = 2 * np.arange(HALF, dtype=np.int64)[None] + 1
    angles = np.pi * ((bins * half_lags) % (4 * BINS)) / (2 * BINS)
    table = np.concatenate([np.cos(angles), np.sin(angles)], 1).astype(ml_dtypes.bfloat16)
    shift = np.pi * np.arange(BINS) / (2 * BINS)
    turn = np.stack([np.cos(shift), np.sin(shift)]).astype(np.float32)
    mirror = np.eye(HALF)[::-1].astype(ml_dtypes.bfloat16)
    return table, turn, mirror


def mult(value, k):
    return pl.multiple_of(value, k)


def gather_kernel(sources, rows_ref, white, out, slots, recv, picked, twin, src, s_sc, r_sc, s_tw, r_tw,
                  s_z, r_z, s_x, r_x, s_t, r_t):
    day = lax.axis_index("day")
    me = lax.axis_index("sta")
    z, x, c, chip = me // 8, (me // 2) % 4, me % 2, me // 2

    def dev(z_to, x_to, c_to):
        return (day, z_to * 8 + x_to * 2 + c_to)

    offsets = [(dz, dx) for dz in (2, 1, 3, 0) for dx in (2, 1, 3, 0) if (dz, dx) != (0, 0)]
    barrier = pltpu.get_barrier_semaphore()
    for dz, dx in offsets:
        pl.semaphore_signal(barrier, inc=1, device_id=dev((z + dz) % 4, (x + dx) % 4, c), device_id_type=MESH)
    pl.semaphore_signal(barrier, inc=1, device_id=dev(z, x, 1 - c), device_id_type=MESH)

    holder, local, rank = [], [], []
    for i in range(16):
        row = rows_ref[sources[i // 8, i % 8]]
        holder.append(row // 16)
        local.append(row % 16)
        count = jnp.int32(0)
        for j in range(i):
            count = count + jnp.where(holder[j] == holder[i], 1, 0)
        rank.append(count)
    ri = lax.broadcasted_iota(jnp.int32, (64, 256), 0)
    ci = lax.broadcasted_iota(jnp.int32, (64, 256), 1)
    target = jnp.full((64, 256), -1, jnp.int32)
    base = 128 * ((ri // 8) % 2) + 32 * (ri // 16) + 16 * ((ri // 4) % 2)
    for i in range(16):
        key = jnp.where(holder[i] == me, rank[i], 99)
        target = jnp.where(ri % 4 == key, base + local[i], target)
    pick = jnp.where(ci == target, 1.0, 0.0).astype(BF16)
    slots[...] = jnp.dot(pick, white[...], preferred_element_type=F32).astype(BF16)
    pl.semaphore_wait(barrier, 16)

    copies = []
    for n, (dz, dx) in enumerate(offsets):
        z_to, x_to = (z + dz) % 4, (x + dx) % 4
        copy = pltpu.make_async_remote_copy(
            src_ref=slots.at[pl.ds(mult(16 * z_to, 16), 16), pl.ds(mult(QUARTER * x_to, 128), QUARTER)],
            dst_ref=recv.at[pl.ds(mult(16 * chip, 16), 16)],
            send_sem=s_sc.at[n],
            recv_sem=r_sc.at[n],
            device_id=dev(z_to, x_to, c),
            device_id_type=MESH,
        )
        copy.start()
        copies.append(copy)
    own = (pl.ds(mult(16 * z, 16), 16), pl.ds(mult(QUARTER * x, 128), QUARTER))
    recv[pl.ds(mult(16 * chip, 16), 16), :] = slots[own]
    target = jnp.full((64, 256), -1, jnp.int32)
    for i in range(16):
        where = jnp.where(holder[i] % 2 == c, 16 * (holder[i] // 2) + rank[i], -1000)
        target = jnp.where(ri % 16 == i, where + 8 * (ri // 32) + 4 * ((ri // 16) % 2), target)
    pick = jnp.where(ci == target, 1.0, 0.0).astype(BF16)
    for copy in copies:
        copy.wait()
    picked[...] = jnp.dot(pick, recv[...], preferred_element_type=F32).astype(BF16)
    copy = pltpu.make_async_remote_copy(
        src_ref=picked.at[pl.ds(mult(32 * (1 - c), 32), 32)],
        dst_ref=twin,
        send_sem=s_tw,
        recv_sem=r_tw,
        device_id=dev(z, x, 1 - c),
        device_id_type=MESH,
    )
    copy.start()
    copy.wait()

    def piece(z_of, x_of):
        return src.at[pl.ds(mult(128 * c + 32 * z_of, 32), 32), pl.ds(mult(QUARTER * x_of, 128), QUARTER)]

    def half(x_of):
        return src.at[pl.ds(mult(128 * c, 128), 128), pl.ds(mult(QUARTER * x_of, 128), QUARTER)]

    def send(ref, s_sem, r_sem, target_id):
        copy = pltpu.make_async_remote_copy(
            src_ref=ref, dst_ref=ref, send_sem=s_sem, recv_sem=r_sem, device_id=target_id, device_id_type=MESH
        )
        copy.start()
        return copy

    piece(z, x)[...] = picked[pl.ds(mult(32 * c, 32), 32), :] + twin[...]

    def send_x(k, z_of):
        return [
            send(piece(z_of, x), s_x.at[k, n], r_x.at[k, n], dev(z, (x + dx) % 4, c))
            for n, dx in enumerate((2, 1, 3))
        ]

    along_z = [send(piece(z, x), s_z.at[n], r_z.at[n], dev((z + dz) % 4, x, c)) for n, dz in enumerate((2, 1, 3))]
    along_x = [send_x(0, z)]
    for n, dz in ((1, 1), (2, 3), (0, 2)):
        along_z[n].wait()
        along_x.append(send_x(1 + n, (z + 4 - dz) % 4))
    across = [send(half(x), s_t.at[0], r_t.at[0], dev(z, x, 1 - c))]
    for n, dx in ((1, 1), (2, 3), (0, 2)):
        for k in range(4):
            along_x[k][n].wait()
        across.append(send(half((x + 4 - dx) % 4), s_t.at[1 + n], r_t.at[1 + n], dev(z, x, 1 - c)))
    for copy in across:
        copy.wait()
    out[...] = src[...]


def gather_sources(sources, station_rows, white):
    sem = pltpu.SemaphoreType.DMA
    return pl.pallas_call(
        gather_kernel,
        out_shape=jax.ShapeDtypeStruct((256, BINS), BF16),
        in_specs=[pl.BlockSpec(memory_space=pltpu.SMEM)] * 2 + [pl.BlockSpec(memory_space=pltpu.VMEM)],
        out_specs=pl.BlockSpec(memory_space=pltpu.VMEM),
        scratch_shapes=[
            pltpu.VMEM((64, BINS), BF16),
            pltpu.VMEM((256, QUARTER), BF16),
            pltpu.VMEM((64, QUARTER), BF16),
            pltpu.VMEM((32, QUARTER), BF16),
            pltpu.VMEM((256, BINS), BF16),
            sem((15,)), sem((15,)), sem, sem, sem((3,)), sem((3,)), sem((4, 3)), sem((4, 3)), sem((4,)), sem((4,)),
        ],
        compiler_params=pltpu.CompilerParams(collective_id=0, has_side_effects=True, vmem_limit_bytes=48 << 20),
    )(sources, station_rows, white)


def correlate_kernel(white, src, table, turn, mirror, weights, out, cross, total, rec_f, src_f):
    step = pl.program_id(0)
    tiles = white.shape[1] // 128

    @pl.when(step == 0)
    def _():
        total[...] = jnp.zeros_like(total)

    for t in range(tiles):
        lanes = pl.ds(t * 128, 128)
        co, si = turn[0:1, lanes], turn[1:2, lanes]
        for h in range(8):
            c = white[pl.ds(32 * h, 16), lanes].astype(F32)
            e = white[pl.ds(32 * h + 16, 16), lanes].astype(F32)
            rec_f[t, h, 0], rec_f[t, h, 1], rec_f[t, h, 2] = c, c - e, c + e
            a = src[pl.ds(32 * h, 16), lanes].astype(F32)
            b = src[pl.ds(32 * h + 16, 16), lanes].astype(F32)
            a_turn, b_turn = a * co + b * si, b * co - a * si
            src_f[t, h, 0], src_f[t, h, 1], src_f[t, h, 2] = a_turn + b_turn, b_turn, a_turn
    for t in range(tiles):
        lanes = pl.ds(t * 128, 128)
        for block in range(4):
            sums = [[None] * 3 for _ in range(4)]
            for h in range(8):
                rec = [rec_f[t, h, k] for k in range(3)]
                for n in range(4):
                    for k in range(3):
                        row = src_f[t, h, k, pl.ds(block * 4 + n, 1), :]
                        term = jnp.broadcast_to(row, (16, 128)) * rec[k]
                        sums[n][k] = term if h == 0 else sums[n][k] + term
            for n in range(4):
                rows = pl.ds(16 * (block * 4 + n), 16)
                cross[0, rows, lanes] = (sums[n][0] - sums[n][1]).astype(BF16)
                cross[1, rows, lanes] = (sums[n][0] - sums[n][2]).astype(BF16)
    total[0] += jnp.dot(cross[0], table[:, 0:HALF], preferred_element_type=F32)
    total[1] += jnp.dot(cross[1], table[:, HALF:], preferred_element_type=F32)

    @pl.when(step == pl.num_programs(0) - 1)
    def _():
        scale = weights[...]
        even, odd = total[0] * scale, total[1] * scale
        out[:, HALF:] = (even - odd).astype(BF16)
        back = jnp.dot((even + odd).astype(BF16), mirror[...], preferred_element_type=F32)
        out[:, 0:HALF] = back.astype(BF16)


def correlate(white, src, weights):
    table, turn, mirror = tables()
    width = QUARTER
    return pl.pallas_call(
        correlate_kernel,
        grid=(BINS // width,),
        out_shape=jax.ShapeDtypeStruct((256, LAGS), BF16),
        in_specs=[
            pl.BlockSpec((256, width), lambda q: (0, q)),
            pl.BlockSpec((256, width), lambda q: (0, q)),
            pl.BlockSpec((width, LAGS), lambda q: (q, 0)),
            pl.BlockSpec((2, width), lambda q: (0, q)),
            pl.BlockSpec((HALF, HALF), lambda q: (0, 0)),
            pl.BlockSpec((256, 1), lambda q: (0, 0)),
        ],
        out_specs=pl.BlockSpec((256, LAGS), lambda q: (0, 0)),
        scratch_shapes=[
            pltpu.VMEM((2, 256, width), BF16),
            pltpu.VMEM((2, 256, HALF), F32),
            pltpu.VMEM((width // 128, 8, 3, 16, 128), F32),
            pltpu.VMEM((width // 128, 8, 3, 16, 128), F32),
        ],
        compiler_params=pltpu.CompilerParams(vmem_limit_bytes=48 << 20),
    )(white, src, jnp.asarray(table), jnp.asarray(turn), jnp.asarray(mirror), weights)


def stack_kernel(term, out, recv, s_sem, r_sem):
    day = lax.axis_index("day")
    sta = lax.axis_index("sta")
    barrier = pltpu.get_barrier_semaphore()
    for n in range(1, 8):
        pl.semaphore_signal(barrier, inc=1, device_id=((day + n) % 8, sta), device_id_type=MESH)
    pl.semaphore_wait(barrier, 7)
    copies = []
    for n in range(1, 8):
        to = (day + n) % 8
        copy = pltpu.make_async_remote_copy(
            src_ref=term.at[:, pl.ds(mult(128 * to, 128), 128)],
            dst_ref=recv.at[n - 1],
            send_sem=s_sem.at[n - 1],
            recv_sem=r_sem.at[n - 1],
            device_id=(to, sta),
            device_id_type=MESH,
        )
        copy.start()
        copies.append(copy)
    for copy in copies:
        copy.wait()
    total = term[:, pl.ds(mult(128 * day, 128), 128)].astype(F32)
    for n in range(7):
        total = total + recv[n].astype(F32)
    out[...] = total


def stack_days(term):
    sem = pltpu.SemaphoreType.DMA
    return pl.pallas_call(
        stack_kernel,
        out_shape=jax.ShapeDtypeStruct((256, 128), F32),
        in_specs=[pl.BlockSpec(memory_space=pltpu.VMEM)],
        out_specs=pl.BlockSpec(memory_space=pltpu.VMEM),
        scratch_shapes=[pltpu.VMEM((7, 256, 128), BF16), sem((7,)), sem((7,))],
        compiler_params=pltpu.CompilerParams(collective_id=1, has_side_effects=True, vmem_limit_bytes=16 << 20),
    )(term)


def shards(spectra, hour_flags, sources, station_rows):
    me = lax.axis_index("sta")
    values = spectra[0].astype(F32)
    power = jnp.mean(values * values, axis=(2, 3))
    valid = hour_flags[0].astype(F32)
    white = (values * (valid / jnp.sqrt(power + EPSILON))[:, :, None, None]).astype(BF16)
    white = white.reshape(16, 4, 2, 2, BINS).transpose(2, 1, 3, 0, 4).reshape(256, BINS)

    rows = station_rows[sources.reshape(-1)]
    holder, local = rows // 16, rows % 16
    mine = (holder == me)[:, None]
    source_valid = lax.psum(jnp.where(mine, valid[local], 0.0), "sta")
    shared = jnp.dot(source_valid, valid.T, precision=lax.Precision.HIGHEST)
    weights = (1.0 / jnp.maximum(shared, 1.0)).reshape(256, 1) * (1.0 / math.sqrt(BINS))

    def general(white):
        kept = jnp.where(mine, white.reshape(16, 16, BINS)[:, local], 0).astype(BF16)
        return lax.psum(kept.reshape(256, BINS), "sta")

    def spread(white):
        return gather_sources(sources, station_rows, white)

    load = jnp.max(jnp.sum((holder[:, None] == holder[None, :]).astype(jnp.int32), axis=1))
    src = lax.cond(load <= SLOTS, spread, general, white)
    term = correlate(white, src, weights)
    return stack_days(term).reshape(16, 16, 128)


def solution(mesh):
    in_specs = (P("day", "sta", None, None, None), P("day", "sta", None), P(), P())
    out_specs = P(None, "sta", "day")
    return jax.shard_map(shards, mesh=mesh, in_specs=in_specs, out_specs=out_specs, check_vma=False)
```

time: 786 us -> 165 us (0.21); the launches traced: 772 us -> 163 us
  matrix products: 290 us -> 0.13 us
  waiting for transfers between devices: 255 us -> 0 us
  Pallas kernels: 0 us -> 65.9 us
  between operations: 63.7 us -> 14.2 us
  other arithmetic: 46.5 us -> 6.95 us
  loops' own time: 27.7 us -> 0.02 us
  local copies, waits for them, and re-layouts: 14.4 us -> 5.3 us
    dot_general x30 -> x1, matrix products: 290 us -> 0.13 us  [shards(): shared = jnp.dot(source_valid, valid.T, precision=lax.Precision.HIGHEST)]
    psum x1 -> x0, waiting for transfers between devices: 220 us -> none  [broadcast(): return lax.psum(kept, axis)]
    pallas_call x0 -> x3, Pallas kernels: none -> 65.9 us  [the longest x1 44.3 us: gather_sources(): pl.pallas_call(gather_kernel, out_shape=jax.ShapeDtypeStruct((256, BINS),...]
    reduce_scatter x2 -> x0, waiting for transfers between devices: 35.1 us -> none  [shards(): stacked = lax.psum_scatter(term, 'day', scatter_dimension=2, tiled=True)]
    another operation x2 -> x1, loops' own time: 27.7 us -> 0.02 us  [shards(): src = lax.cond(load <= SLOTS, spread, general, white)]
    reduce_sum x2, other arithmetic: 26.6 us -> 2.7 us  [the longest x1 2.52 us: shards(): power = jnp.mean(values * values, axis=(2, 3))]
    unnamed x40 -> x13, local copies, waits for them, and re-layouts: 8.76 us -> 0.69 us
  transfers between devices with their start and end apart: 3 -> 0, of which waited for: 2 -> 0; matrix products, arithmetic and copies ran while one was open for 20% -> 0% of each run, Pallas kernels for 0% -> 0%
where the time goes in v1:
time: 165 us; the launch traced here: 163 us
  blocking collectives  70.5 us (43%)
  Pallas kernels  65.9 us (40%)
  between operations  14.2 us (9%)
  other arithmetic  6.95 us (4%)
  local copies, waits for them, and re-layouts  5.3 us (3%)
    psum x1, blocking collectives, shards(): source_valid = lax.psum(jnp.where(mine, valid[local], 0.0), 'sta')  70.5 us
    pallas_call x1, Pallas kernels, gather_sources(): pl.pallas_call(gather_kernel, out_shape=jax.ShapeDtypeStruct((256, BINS),...  44.3 us
    pallas_call x1, Pallas kernels, correlate(): pl.pallas_call(correlate_kernel, grid=(BINS // width,), out_shape=jax.Sha...  11.1 us
    pallas_call x1, Pallas kernels, stack_days(): pl.pallas_call(stack_kernel, out_shape=jax.ShapeDtypeStruct((256, 128), F...  10.6 us

profile of v1, /device:TPU:1, one launch (start us, length us, event | category | flops | bytes accessed | tf_op | source)
XLA Modules:
  0.0 163.1 jit_solution(915179508153867466)
XLA Ops:
  6.5 0.0 copy-start.3
  6.5 0.9 reshape.178
  7.4 1.3 gather_fusion.1
  8.8 0.7 convert_bitcast_fusion
  9.5 2.5 %multiply_reduce_fusion = f32[16,8]{0,1:T(8,128)S(1)} fusion(bf16[1,16,8,2,3584]{4,3,2,1,0:T(2,128)(2,1)} %param.9), kind=kLoop, calls=%fused_computation.11 | loop fusion | flops 2752384 | bytes 1835520 | tf_op jit(solution)/shard_map/reduce_sum | solution.py:278
  12.1 0.0 copy-done.3
  12.1 1.1 copy_convert_fusion
  13.2 1.6 fusion
  14.8 0.2 convert_reduce_fusion
  15.0 0.7 reduce_max.9
  16.4 0.0 copy-start.2
  16.4 0.0 copy-start.5
  16.4 1.6 copy.23
  18.0 0.0 copy-done.2
  18.0 0.0 copy-done.5
  18.1 0.0 copy-start.4
  18.1 0.0 copy-start
  18.1 0.0 copy-start.1
  18.1 44.3 %conditional.1 = (bf16[256,3584]{1,0:T(8,128)(2,1)}) conditional(s32[]{:T(128)} %convert_element_type.42, (s32[16,1]{0,1:T(1,128)S(1)}, pred[16,1]{0,1:T(4,128)(4,1)S(1)}, s32[16,1]{0,1:T(1,128)S(1)}, pred[16,1]{0,1:T(4,128)(4,1)S(1)}, s32[]{:T(128)}, /*index=5*/bf16[2,4,2,16,3584]{4,3,2,0,1:T(8,128)(2,1)}, s32[16]{0:T(128)S(1)}) %tuple.28, ...), branch_computations={%region_3.5_spmd, %region_5.6_spmd} | conditional | flops 1836304 | bytes 29365748 | solution.py:298
  18.1 44.3 %branch_1_fun.1 = bf16[256,3584]{1,0:T(8,128)(2,1)} custom-call(s32[2,8]{1,0:T(2,128)S(1)} %get-tuple-element.66.sources, s32[512]{0:T(512)S(1)} %get-tuple-element.67.rows_ref, bf16[256,3584]{1,0:T(8,128)(2,1)S(1)} %get-tuple-element.68.white), custom_call_target="tpu_custom_call" | custom-call | tf_op jit(solution)/shard_map/cond/branch_1_fun/pallas_call | solution.py:146
  62.4 0.1 copy.25
  62.5 0.6 gather_fusion.2
  63.1 0.1 broadcast_select_fusion
  63.1 70.5 %psum.14 = f32[16,8]{1,0:T(8,128)S(1)} all-reduce(f32[16,8]{1,0:T(8,128)S(1)} %broadcast_select_fusion), channel_id=1, replica_groups=mesh['day'=8,'sta'=32] {'sta'}, use_global_device_ids=true, to_apply=%region_6.7 | all-reduce | flops 128 | bytes 1024 | tf_op jit(solution)/shard_map/psum | solution.py:286
  133.6 0.0 copy-done.4
  133.7 0.1 fusion.2
  133.8 0.1 mul.27.weights
  133.9 0.0 copy-done
  133.9 0.0 copy-done.1
  133.9 11.1 %shard_map.73.term = bf16[256,1024]{1,0:T(8,128)(2,1)S(1)} custom-call(bf16[256,3584]{1,0:T(8,128)(2,1)S(1)} %bitcast.38, bf16[256,3584]{1,0:T(8,128)(2,1)} %get-tuple-element.99.src, bf16[3584,1024]{1,0:T(8,128)(2,1)} %constant.71.clone.table, f32[2,3584]{1,0:T(2,128)S(1)} %copy-done.1, bf16[512,512]{1,0:T(8,128)(2,1)S(1)} %copy-done, f32[256,1]{1,0:T(8,128)S(1)} %mul.27.weights), custom_call_target="tpu_custom_call" | custom-call | tf_op jit(solution)/shard_map/pallas_call | solution.py:212
  145.0 10.6 %shard_map.74 = f32[256,128]{1,0:T(8,128)S(1)} custom-call(bf16[256,1024]{1,0:T(8,128)(2,1)S(1)} %shard_map.73.term), custom_call_target="tpu_custom_call" | custom-call | tf_op jit(solution)/shard_map/pallas_call | solution.py:265
  155.6 0.7 copy.34
  (8 shorter events, 0.1 us)
Async XLA Ops:
  6.5 5.5 %copy-start.3 = (bf16[1,16,8,2,3584]{4,3,2,1,0:T(2,128)(2,1)S(1)}, bf16[1,16,8,2,3584]{4,3,2,1,0:T(2,128)(2,1)}, u32[]{:S(2)}) copy-start(bf16[1,16,8,2,3584]{4,3,2,1,0:T(2,128)(2,1)} %param.9) | copy-start | bytes 5505028
  16.4 1.7 %copy-start.2 = (s32[512]{0:T(512)S(1)}, s32[512]{0:T(512)}, u32[]{:S(2)}) copy-start(s32[512]{0:T(512)} %param.12) | copy-start | bytes 6148
  16.4 1.7 %copy-start.5 = (s32[2,8]{1,0:T(2,128)S(1)}, s32[2,8]{1,0:T(2,128)}, u32[]{:S(2)}) copy-start(s32[2,8]{1,0:T(2,128)} %param.11) | copy-start | bytes 196
  18.1 115.6 %copy-start.4 = (s32[1,16,8]{1,2,0:T(8,128)S(1)}, s32[1,16,8]{1,2,0:T(8,128)}, u32[]{:S(2)}) copy-start(s32[1,16,8]{1,2,0:T(8,128)} %param.10) | copy-start | bytes 1540
  18.1 115.8 %copy-start = (bf16[512,512]{1,0:T(8,128)(2,1)S(1)}, bf16[512,512]{1,0:T(8,128)(2,1)}, u32[]{:S(2)}) copy-start(bf16[512,512]{1,0:T(8,128)(2,1)} %constant.73.clone.mirror) | copy-start | bytes 1572868
  18.1 115.8 %copy-start.1 = (f32[2,3584]{1,0:T(2,128)S(1)}, f32[2,3584]{1,0:T(2,128)}, u32[]{:S(2)}) copy-start(f32[2,3584]{1,0:T(2,128)} %constant.72.clone.turn) | copy-start | bytes 86020

commit v2 on v1

v2 whole, which is shorter than its diff:
```python
import functools
import math

import jax
import jax.numpy as jnp
import ml_dtypes
import numpy as np
from jax import lax
from jax.experimental import pallas as pl
from jax.experimental.pallas import tpu as pltpu
from jax.sharding import PartitionSpec as P

BINS = 3584
LAGS = 1024
HALF = LAGS // 2
QUARTER = BINS // 4
EPSILON = 1e-06
SLOTS = 4
MESH = pl.DeviceIdType.MESH
BF16 = jnp.bfloat16
F32 = jnp.float32


def tables():
    bins = np.arange(BINS, dtype=np.int64)[:, None]
    half_lags = 2 * np.arange(HALF, dtype=np.int64)[None] + 1
    angles = np.pi * ((bins * half_lags) % (4 * BINS)) / (2 * BINS)
    table = np.concatenate([np.cos(angles), np.sin(angles)], 1).astype(ml_dtypes.bfloat16)
    shift = np.pi * np.arange(BINS) / (2 * BINS)
    turn = np.stack([np.cos(shift), np.sin(shift)]).astype(np.float32)
    mirror = np.eye(HALF)[::-1].astype(ml_dtypes.bfloat16)
    return table, turn, mirror


def mult(value, k):
    return pl.multiple_of(value, k)


def correlate_kernel(white, src, table, turn, mirror, weights, out, cross, total, rec_f, src_f):
    step = pl.program_id(0)
    tiles = white.shape[1] // 128

    @pl.when(step == 0)
    def _():
        total[...] = jnp.zeros_like(total)

    for t in range(tiles):
        lanes = pl.ds(t * 128, 128)
        co, si = turn[0:1, lanes], turn[1:2, lanes]
        for h in range(8):
            c = white[pl.ds(32 * h, 16), lanes].astype(F32)
            e = white[pl.ds(32 * h + 16, 16), lanes].astype(F32)
            rec_f[t, h, 0], rec_f[t, h, 1], rec_f[t, h, 2] = c, c - e, c + e
            a = src[pl.ds(32 * h, 16), lanes].astype(F32)
            b = src[pl.ds(32 * h + 16, 16), lanes].astype(F32)
            a_turn, b_turn = a * co + b * si, b * co - a * si
            src_f[t, h, 0], src_f[t, h, 1], src_f[t, h, 2] = a_turn + b_turn, b_turn, a_turn
    for t in range(tiles):
        lanes = pl.ds(t * 128, 128)
        for block in range(4):
            sums = [[None] * 3 for _ in range(4)]
            for h in range(8):
                rec = [rec_f[t, h, k] for k in range(3)]
                for n in range(4):
                    for k in range(3):
                        row = src_f[t, h, k, pl.ds(block * 4 + n, 1), :]
                        term = jnp.broadcast_to(row, (16, 128)) * rec[k]
                        sums[n][k] = term if h == 0 else sums[n][k] + term
            for n in range(4):
                rows = pl.ds(16 * (block * 4 + n), 16)
                cross[0, rows, lanes] = (sums[n][0] - sums[n][1]).astype(BF16)
                cross[1, rows, lanes] = (sums[n][0] - sums[n][2]).astype(BF16)
    total[0] += jnp.dot(cross[0], table[:, 0:HALF], preferred_element_type=F32)
    total[1] += jnp.dot(cross[1], table[:, HALF:], preferred_element_type=F32)

    @pl.when(step == pl.num_programs(0) - 1)
    def _():
        scale = weights[...]
        even, odd = total[0] * scale, total[1] * scale
        out[:, HALF:] = (even - odd).astype(BF16)
        back = jnp.dot((even + odd).astype(BF16), mirror[...], preferred_element_type=F32)
        out[:, 0:HALF] = back.astype(BF16)


def correlate(white, src, weights):
    table, turn, mirror = tables()
    width = QUARTER
    return pl.pallas_call(
        correlate_kernel,
        grid=(BINS // width,),
        out_shape=jax.ShapeDtypeStruct((256, LAGS), BF16),
        in_specs=[
            pl.BlockSpec((256, width), lambda q: (0, q)),
            pl.BlockSpec((256, width), lambda q: (0, q)),
            pl.BlockSpec((width, LAGS), lambda q: (q, 0)),
            pl.BlockSpec((2, width), lambda q: (0, q)),
            pl.BlockSpec((HALF, HALF), lambda q: (0, 0)),
            pl.BlockSpec((256, 1), lambda q: (0, 0)),
        ],
        out_specs=pl.BlockSpec((256, LAGS), lambda q: (0, 0)),
        scratch_shapes=[
            pltpu.VMEM((2, 256, width), BF16),
            pltpu.VMEM((2, 256, HALF), F32),
            pltpu.VMEM((width // 128, 8, 3, 16, 128), F32),
            pltpu.VMEM((width // 128, 8, 3, 16, 128), F32),
        ],
        compiler_params=pltpu.CompilerParams(vmem_limit_bytes=48 << 20),
    )(white, src, jnp.asarray(table), jnp.asarray(turn), jnp.asarray(mirror), weights)


def fused_kernel(sources, rows_ref, spectra, flags, table_hbm, turn, mirror, out, load, table, white, slots, recv, picked,
                 twin, src, valid, cross, total, rec_f, src_f, days, daily, s_tab, s_sc, r_sc, s_tw, r_tw, s_z, r_z,
                 s_x, r_x, s_t, r_t, s_fz, r_fz, s_fx, r_fx, s_ft, r_ft, s_d, r_d):
    day = lax.axis_index("day")
    me = lax.axis_index("sta")
    z, x, c, chip = me // 8, (me // 2) % 4, me % 2, me // 2

    def dev(z_to, x_to, c_to):
        return (day, z_to * 8 + x_to * 2 + c_to)

    def remote(source, target, s_sem, r_sem, device):
        copy = pltpu.make_async_remote_copy(
            src_ref=source, dst_ref=target, send_sem=s_sem, recv_sem=r_sem, device_id=device, device_id_type=MESH
        )
        copy.start()
        return copy

    offsets = [(dz, dx) for dz in (2, 1, 3, 0) for dx in (2, 1, 3, 0) if (dz, dx) != (0, 0)]
    barrier = pltpu.get_barrier_semaphore()
    for dz, dx in offsets:
        pl.semaphore_signal(barrier, inc=1, device_id=dev((z + dz) % 4, (x + dx) % 4, c), device_id_type=MESH)
    pl.semaphore_signal(barrier, inc=1, device_id=dev(z, x, 1 - c), device_id_type=MESH)
    for n in range(1, 8):
        pl.semaphore_signal(barrier, inc=1, device_id=((day + n) % 8, me), device_id_type=MESH)
    table_copy = pltpu.make_async_copy(table_hbm, table, s_tab)
    table_copy.start()

    ri = lax.broadcasted_iota(jnp.int32, (256, 256), 0)
    ci = lax.broadcasted_iota(jnp.int32, (256, 256), 1)
    natural = (ri % 16) * 16 + 4 * ((ri // 32) % 4) + 2 * (ri // 128) + (ri // 16) % 2
    order = jnp.where(ci == natural, 1.0, 0.0).astype(BF16)
    power = jnp.zeros((256, 128), F32)
    for k in range(BINS // 256):
        lanes = pl.ds(256 * k, 256)
        values = jnp.dot(order, spectra[:, lanes], preferred_element_type=F32)
        white[:, lanes] = values.astype(BF16)
        squares = values * values
        power = power + squares[:, :128] + squares[:, 128:]
    power = jnp.sum(power, axis=1, keepdims=True)
    flag = flags[...].astype(F32)
    for h in range(8):
        hour = 2 * (h % 4) + h // 4
        mean = (power[32 * h:32 * h + 16] + power[32 * h + 16:32 * h + 32]) * (1.0 / (2 * BINS))
        scale = flag[:, hour:hour + 1] / jnp.sqrt(mean + EPSILON)
        for p in range(2):
            rows = pl.ds(32 * h + 16 * p, 16)
            white[rows, :] = (white[rows, :].astype(F32) * scale).astype(BF16)
    wide = jnp.concatenate([flag, jnp.zeros((16, 120), F32)], axis=1)
    own_flags = pl.ds(mult(256 * c + 64 * x + 16 * z, 16), 16)
    valid[own_flags, :] = wide.astype(BF16)

    holder, local, rank = [], [], []
    most = jnp.int32(0)
    for i in range(16):
        row = rows_ref[sources[i // 8, i % 8]]
        holder.append(row // 16)
        local.append(row % 16)
        count = jnp.int32(0)
        for j in range(i):
            count = count + jnp.where(holder[j] == holder[i], 1, 0)
        rank.append(count)
        most = jnp.maximum(most, count + 1)
    load[0] = most
    ri, ci = ri[:64], ci[:64]
    target = jnp.full((64, 256), -1, jnp.int32)
    base = 128 * ((ri // 8) % 2) + 32 * (ri // 16) + 16 * ((ri // 4) % 2)
    for i in range(16):
        key = jnp.where(holder[i] == me, rank[i], 99)
        target = jnp.where(ri % 4 == key, base + local[i], target)
    pick = jnp.where(ci == target, 1.0, 0.0).astype(BF16)
    slots[...] = jnp.dot(pick, white[...], preferred_element_type=F32).astype(BF16)
    pl.semaphore_wait(barrier, 23)

    copies = []
    for n, (dz, dx) in enumerate(offsets):
        z_to, x_to = (z + dz) % 4, (x + dx) % 4
        copies.append(
            remote(
                slots.at[pl.ds(mult(16 * z_to, 16), 16), pl.ds(mult(QUARTER * x_to, 128), QUARTER)],
                recv.at[pl.ds(mult(16 * chip, 16), 16)],
                s_sc.at[n],
                r_sc.at[n],
                dev(z_to, x_to, c),
            )
        )
    ref = valid.at[own_flags]
    flag_z = [remote(ref, ref, s_fz.at[n], r_fz.at[n], dev((z + 1 + n) % 4, x, c)) for n in range(3)]
    recv[pl.ds(mult(16 * chip, 16), 16), :] = slots[
        pl.ds(mult(16 * z, 16), 16), pl.ds(mult(QUARTER * x, 128), QUARTER)
    ]
    target = jnp.full((64, 256), -1, jnp.int32)
    for i in range(16):
        where = jnp.where(holder[i] % 2 == c, 16 * (holder[i] // 2) + rank[i], -1000)
        target = jnp.where(ri % 16 == i, where + 8 * (ri // 32) + 4 * ((ri // 16) % 2), target)
    pick = jnp.where(ci == target, 1.0, 0.0).astype(BF16)

    def receiver_planes(t, carry):
        lanes = pl.ds(mult(t * 128, 128), 128)
        for h in range(8):
            cosine = white[pl.ds(32 * h, 16), lanes].astype(F32)
            sine = white[pl.ds(32 * h + 16, 16), lanes].astype(F32)
            rec_f[t, h, 0] = cosine
            rec_f[t, h, 1] = cosine - sine
            rec_f[t, h, 2] = cosine + sine
        return carry

    lax.fori_loop(0, BINS // 128, receiver_planes, 0)
    total[...] = jnp.zeros_like(total)

    for copy in flag_z:
        copy.wait()
    ref = valid.at[pl.ds(mult(256 * c + 64 * x, 64), 64)]
    flag_x = [remote(ref, ref, s_fx.at[n], r_fx.at[n], dev(z, (x + 1 + n) % 4, c)) for n in range(3)]
    for copy in copies:
        copy.wait()
    picked[...] = jnp.dot(pick, recv[...], preferred_element_type=F32).astype(BF16)
    copy = remote(picked.at[pl.ds(mult(32 * (1 - c), 32), 32)], twin, s_tw, r_tw, dev(z, x, 1 - c))
    copy.wait()

    def piece(z_of, x_of):
        return src.at[pl.ds(mult(128 * c + 32 * z_of, 32), 32), pl.ds(mult(QUARTER * x_of, 128), QUARTER)]

    def half(x_of):
        return src.at[pl.ds(mult(128 * c, 128), 128), pl.ds(mult(QUARTER * x_of, 128), QUARTER)]

    def send(ref, s_sem, r_sem, device):
        return remote(ref, ref, s_sem, r_sem, device)

    piece(z, x)[...] = picked[pl.ds(mult(32 * c, 32), 32), :] + twin[...]

    def send_x(k, z_of):
        return [
            send(piece(z_of, x), s_x.at[k, n], r_x.at[k, n], dev(z, (x + dx) % 4, c))
            for n, dx in enumerate((2, 1, 3))
        ]

    along_z = [send(piece(z, x), s_z.at[n], r_z.at[n], dev((z + dz) % 4, x, c)) for n, dz in enumerate((2, 1, 3))]
    along_x = [send_x(0, z)]
    for copy in flag_x:
        copy.wait()
    ref = valid.at[pl.ds(mult(256 * c, 256), 256)]
    flag_t = remote(ref, ref, s_ft, r_ft, dev(z, x, 1 - c))
    for n, dz in ((1, 1), (2, 3), (0, 2)):
        along_z[n].wait()
        along_x.append(send_x(1 + n, (z + 4 - dz) % 4))

    def correlate_quarter(q):
        def tile(t, carry):
            all_lanes = pl.ds(mult(QUARTER * q + 128 * t, 128), 128)
            lanes = pl.ds(mult(128 * t, 128), 128)
            at = 7 * q + t
            co, si = turn[0:1, all_lanes], turn[1:2, all_lanes]
            for h in range(8):
                a = src[pl.ds(32 * h, 16), all_lanes].astype(F32)
                b = src[pl.ds(32 * h + 16, 16), all_lanes].astype(F32)
                a_turn, b_turn = a * co + b * si, b * co - a * si
                src_f[h, 0], src_f[h, 1], src_f[h, 2] = a_turn + b_turn, b_turn, a_turn
            for block in range(4):
                sums = [[None] * 3 for _ in range(4)]
                for h in range(8):
                    rec = [rec_f[at, h, k] for k in range(3)]
                    for n in range(4):
                        for k in range(3):
                            row = src_f[h, k, pl.ds(block * 4 + n, 1), :]
                            term = jnp.broadcast_to(row, (16, 128)) * rec[k]
                            sums[n][k] = term if h == 0 else sums[n][k] + term
                for n in range(4):
                    rows = pl.ds(16 * (block * 4 + n), 16)
                    cross[0, rows, lanes] = (sums[n][0] - sums[n][1]).astype(BF16)
                    cross[1, rows, lanes] = (sums[n][0] - sums[n][2]).astype(BF16)
            return carry

        lax.fori_loop(0, 7, tile, 0)
        bins = pl.ds(mult(QUARTER * q, 128), QUARTER)
        total[0] += jnp.dot(cross[0], table[bins, 0:HALF], preferred_element_type=F32)
        total[1] += jnp.dot(cross[1], table[bins, HALF:], preferred_element_type=F32)

    across = [send(half(x), s_t.at[0], r_t.at[0], dev(z, x, 1 - c))]
    flag_t.wait()
    ri = lax.broadcasted_iota(jnp.int32, (256, 512), 0)
    ci = lax.broadcasted_iota(jnp.int32, (256, 512), 1)
    target = jnp.full((256, 512), -1, jnp.int32)
    for i in range(16):
        where = 256 * (holder[i] % 2) + 64 * ((holder[i] // 2) % 4) + 16 * (holder[i] // 8) + local[i]
        target = jnp.where(ri // 16 == i, where, target)
    choose = jnp.where(ci == target, 1.0, 0.0).astype(BF16)
    shared = jnp.dot(choose, valid[...], preferred_element_type=F32) * jnp.concatenate([wide] * 16, axis=0)
    shared = jnp.sum(shared, axis=1, keepdims=True)
    scale = (1.0 / jnp.maximum(shared, 1.0)) * (1.0 / math.sqrt(BINS))

    table_copy.wait()
    across[0].wait()
    correlate_quarter(x)
    for n, dx in ((1, 1), (2, 3), (0, 2)):
        for k in range(4):
            along_x[k][n].wait()
        copy = send(half((x + 4 - dx) % 4), s_t.at[1 + n], r_t.at[1 + n], dev(z, x, 1 - c))
        copy.wait()
        correlate_quarter((x + 4 - dx) % 4)

    even, odd = total[0] * scale, total[1] * scale
    for n in range(4):
        daily[4 + n] = (even - odd)[:, 128 * n:128 * n + 128].astype(BF16)
    back = jnp.dot((even + odd).astype(BF16), mirror[...], preferred_element_type=F32)
    for n in range(4):
        daily[n] = back[:, 128 * n:128 * n + 128].astype(BF16)
    copies = []
    for n in (4, 3, 5, 2, 6, 1, 7):
        to = (day + n) % 8
        copies.append(remote(daily.at[to], days.at[n - 1], s_d.at[n - 1], r_d.at[n - 1], (to, me)))
    for copy in copies:
        copy.wait()
    result = daily[day].astype(F32)
    for n in range(7):
        result = result + days[n].astype(F32)
    out[...] = result


def fused(sources, station_rows, spectra, flags):
    table, turn, mirror = tables()
    sem = pltpu.SemaphoreType.DMA
    vmem = pl.BlockSpec(memory_space=pltpu.VMEM)
    smem = pl.BlockSpec(memory_space=pltpu.SMEM)
    return pl.pallas_call(
        fused_kernel,
        out_shape=(jax.ShapeDtypeStruct((256, 128), F32), jax.ShapeDtypeStruct((1,), jnp.int32)),
        in_specs=[smem, smem, vmem, vmem, pl.BlockSpec(memory_space=pl.ANY), vmem, vmem],
        out_specs=(vmem, smem),
        scratch_shapes=[
            pltpu.VMEM((BINS, LAGS), BF16),
            pltpu.VMEM((256, BINS), BF16),
            pltpu.VMEM((64, BINS), BF16),
            pltpu.VMEM((256, QUARTER), BF16),
            pltpu.VMEM((64, QUARTER), BF16),
            pltpu.VMEM((32, QUARTER), BF16),
            pltpu.VMEM((256, BINS), BF16),
            pltpu.VMEM((512, 128), BF16),
            pltpu.VMEM((2, 256, QUARTER), BF16),
            pltpu.VMEM((2, 256, HALF), F32),
            pltpu.VMEM((BINS // 128, 8, 3, 16, 128), F32),
            pltpu.VMEM((8, 3, 16, 128), F32),
            pltpu.VMEM((7, 256, 128), BF16),
            pltpu.VMEM((8, 256, 128), BF16),
            sem,
            sem((15,)), sem((15,)), sem, sem, sem((3,)), sem((3,)), sem((4, 3)), sem((4, 3)), sem((4,)), sem((4,)),
            sem((3,)), sem((3,)), sem((3,)), sem((3,)), sem, sem, sem((7,)), sem((7,)),
        ],
        compiler_params=pltpu.CompilerParams(collective_id=0, has_side_effects=True, vmem_limit_bytes=52 << 20),
    )(sources, station_rows, spectra, flags, jnp.asarray(table), jnp.asarray(turn), jnp.asarray(mirror))


def general(spectra, hour_flags, sources, station_rows):
    me = lax.axis_index("sta")
    values = spectra[0].astype(F32)
    power = jnp.mean(values * values, axis=(2, 3))
    valid = hour_flags[0].astype(F32)
    white = (values * (valid / jnp.sqrt(power + EPSILON))[:, :, None, None]).astype(BF16)
    white = white.reshape(16, 16, BINS).transpose(1, 0, 2)
    rows = station_rows[sources.reshape(-1)]
    holder, local = rows // 16, rows % 16
    mine = (holder == me)[:, None]
    source_valid = lax.psum(jnp.where(mine, valid[local], 0.0), "sta")
    shared = jnp.dot(source_valid, valid.T, precision=lax.Precision.HIGHEST)
    weights = (1.0 / jnp.maximum(shared, 1.0)).reshape(256, 1) * (1.0 / math.sqrt(BINS))
    kept = jnp.where(mine, white[:, local], 0).astype(BF16)
    src = lax.psum(kept.reshape(256, BINS), "sta")
    term = correlate(white.reshape(256, BINS), src, weights).astype(F32)
    return lax.psum_scatter(term, "day", scatter_dimension=1, tiled=True)


def shards(spectra, hour_flags, sources, station_rows):
    stacked, load = fused(sources, station_rows, spectra.reshape(256, BINS), hour_flags[0])
    stacked = lax.cond(
        load[0] <= SLOTS,
        lambda *args: stacked,
        general,
        spectra, hour_flags, sources, station_rows,
    )
    return stacked.reshape(16, 16, 128)


def solution(mesh):
    in_specs = (P("day", "sta", None, None, None), P("day", "sta", None), P(), P())
    out_specs = P(None, "sta", "day")
    return jax.shard_map(shards, mesh=mesh, in_specs=in_specs, out_specs=out_specs, check_vma=False)
```

time: 165 us -> 83.1 us (0.50); the launches traced: 163 us -> 82.9 us
  blocking collectives: 70.5 us -> 0 us
  other arithmetic: 6.95 us -> 0 us
  Pallas kernels: 65.9 us -> 63.9 us
    psum x1 -> x0, blocking collectives: 70.5 us -> none  [shards(): source_valid = lax.psum(jnp.where(mine, valid[local], 0.0), 'sta')]
    reshape x1, local copies, waits for them, and re-layouts: 0.89 us -> 4.12 us  [shards(): spectra.reshape(256, BINS)]
    reduce_sum x2 -> x0, other arithmetic: 2.7 us -> none  [the longest x1 2.52 us: shards(): power = jnp.mean(values * values, axis=(2, 3))]
    pallas_call x3 -> x1, Pallas kernels: 65.9 us -> 63.9 us  [fused(): pl.pallas_call(fused_kernel, out_shape=(jax.ShapeDtypeStruct((256, 128),...]
    gather x2 -> x0, local copies, waits for them, and re-layouts: 1.9 us -> none  [the longest x1 1.34 us: shards(): rows = station_rows[sources.reshape(-1)]]
    convert_element_type x2 -> x0, other arithmetic: 1.76 us -> none  [the longest x1 1.07 us: shards(): values = spectra[0].astype(F32)]
where the time goes in v2:
time: 83.1 us; the launch traced here: 82.9 us
  Pallas kernels  63.9 us (77%)
  between operations  14 us (17%)
  local copies, waits for them, and re-layouts  4.87 us (6%)
    pallas_call x1, Pallas kernels, fused(): pl.pallas_call(fused_kernel, out_shape=(jax.ShapeDtypeStruct((256, 128),...  63.9 us
    reshape x1, local copies, waits for them, and re-layouts, shards(): spectra.reshape(256, BINS)  4.12 us

profile of v2, /device:TPU:1, one launch (start us, length us, event | category | flops | bytes accessed | tf_op | source)
XLA Modules:
  0.0 82.9 jit_solution(8351217910605219122)
XLA Ops:
  6.5 0.0 copy-start.4
  6.5 0.0 copy-start.5
  6.5 0.0 copy-start.7
  6.5 0.0 copy-start.1
  6.5 0.0 copy-start.6
  6.5 4.1 %reshape.149.spectra = bf16[256,3584]{1,0:T(8,128)(2,1)S(1)} reshape(bf16[1,16,8,2,3584]{4,3,2,1,0:T(2,128)(2,1)} %param.12) | data formatting | bytes 3670016 | tf_op jit(solution)/shard_map/reshape | solution.py:382
  10.7 0.0 copy-done.6
  10.7 0.1 copy.42.flags
  10.8 0.0 copy-done.4
  10.8 0.0 copy-done.5
  10.8 0.0 copy-done.7
  10.8 0.0 copy-done.1
  10.8 63.9 %shard_map.102 = (f32[256,128]{1,0:T(8,128)S(1)}, s32[1]{0:T(128)}) custom-call(s32[2,8]{1,0:T(2,128)S(1)} %copy-done.7, s32[512]{0:T(512)S(1)} %copy-done.1, bf16[256,3584]{1,0:T(8,128)(2,1)S(1)} %reshape.149.spectra, s32[16,8]{1,0:T(8,128)S(1)} %copy.42.flags, bf16[3584,1024]{1,0:T(8,128)(2,1)} %constant.59.clone.table_hbm, f32[2,3584]{1,0:T(2,128)S(1)} %copy-done.5, ...), custom_call_target="tpu_custom_call" | custom-call | tf_op jit(solution)/shard_map/pallas_call | solution.py:334
  75.2 0.9 %conditional.1 = (f32[16,16,128]{2,1,0:T(8,128)}) conditional(s32[]{:T(128)} %bitcast.12, (bf16[1,16,8,2,3584]{4,3,2,1,0:T(2,128)(2,1)}, s32[1,16,8]{1,2,0:T(8,128)S(1)}, s32[2,8]{1,0:T(2,128)S(1)}, s32[512]{0:T(512)S(1)}, bf16[3584,1024]{1,0:T(8,128)(2,1)}, /*index=5*/f32[2,3584]{1,0:T(2,128)S(1)}, bf16[512,512]{1,0:T(8,128)(2,1)S(1)}) %tuple.27, ...), branch_computations={%region_0.5_spmd, %region_5.6_spmd} | conditional | flops 6713490 | bytes 65694324 | solution.py:383
  75.4 0.7 copy.45
Async XLA Ops:
  6.5 4.2 %copy-start.4 = (bf16[512,512]{1,0:T(8,128)(2,1)S(1)}, bf16[512,512]{1,0:T(8,128)(2,1)}, u32[]{:S(2)}) copy-start(bf16[512,512]{1,0:T(8,128)(2,1)} %constant.61.clone.mirror) | copy-start | bytes 1572868
  6.5 4.2 %copy-start.5 = (f32[2,3584]{1,0:T(2,128)S(1)}, f32[2,3584]{1,0:T(2,128)}, u32[]{:S(2)}) copy-start(f32[2,3584]{1,0:T(2,128)} %constant.60.clone.turn) | copy-start | bytes 86020
  6.5 4.2 %copy-start.7 = (s32[2,8]{1,0:T(2,128)S(1)}, s32[2,8]{1,0:T(2,128)}, u32[]{:S(2)}) copy-start(s32[2,8]{1,0:T(2,128)} %sources.1) | copy-start | bytes 196
  6.5 4.2 %copy-start.1 = (s32[512]{0:T(512)S(1)}, s32[512]{0:T(512)}, u32[]{:S(2)}) copy-start(s32[512]{0:T(512)} %rows_ref.1) | copy-start | bytes 6148
  6.5 4.1 %copy-start.6 = (s32[1,16,8]{1,2,0:T(8,128)S(1)}, s32[1,16,8]{1,2,0:T(8,128)}, u32[]{:S(2)}) copy-start(s32[1,16,8]{1,2,0:T(8,128)} %param.13) | copy-start | bytes 1540

commit v3 on v2

--- a/solution.py
+++ b/solution.py
@@ -108,8 +108,8 @@
     )(white, src, jnp.asarray(table), jnp.asarray(turn), jnp.asarray(mirror), weights)
 
 
-def fused_kernel(sources, rows_ref, spectra, flags, table_hbm, turn, mirror, out, load, table, white, slots, recv, picked,
-                 twin, src, valid, cross, total, rec_f, src_f, days, daily, s_tab, s_sc, r_sc, s_tw, r_tw, s_z, r_z,
+def fused_kernel(sources, rows_ref, spectra_hbm, flags, table_hbm, turn, mirror, out, load, spectra, table, white, slots, recv, picked,
+                 twin, src, valid, cross, total, rec_f, src_f, days, daily, s_spec, s_tab, s_sc, r_sc, s_tw, r_tw, s_z, r_z,
                  s_x, r_x, s_t, r_t, s_fz, r_fz, s_fx, r_fx, s_ft, r_ft, s_d, r_d):
     day = lax.axis_index("day")
     me = lax.axis_index("sta")
@@ -125,6 +125,8 @@
         copy.start()
         return copy
 
+    spectra_copy = pltpu.make_async_copy(spectra_hbm, spectra, s_spec)
+    spectra_copy.start()
     offsets = [(dz, dx) for dz in (2, 1, 3, 0) for dx in (2, 1, 3, 0) if (dz, dx) != (0, 0)]
     barrier = pltpu.get_barrier_semaphore()
     for dz, dx in offsets:
@@ -140,9 +142,10 @@
     natural = (ri % 16) * 16 + 4 * ((ri // 32) % 4) + 2 * (ri // 128) + (ri // 16) % 2
     order = jnp.where(ci == natural, 1.0, 0.0).astype(BF16)
     power = jnp.zeros((256, 128), F32)
+    spectra_copy.wait()
     for k in range(BINS // 256):
         lanes = pl.ds(256 * k, 256)
-        values = jnp.dot(order, spectra[:, lanes], preferred_element_type=F32)
+        values = jnp.dot(order, spectra[:, :, :, lanes].reshape(256, 256), preferred_element_type=F32)
         white[:, lanes] = values.astype(BF16)
         squares = values * values
         power = power + squares[:, :128] + squares[:, 128:]
@@ -331,12 +334,14 @@
     sem = pltpu.SemaphoreType.DMA
     vmem = pl.BlockSpec(memory_space=pltpu.VMEM)
     smem = pl.BlockSpec(memory_space=pltpu.SMEM)
+    hbm = pl.BlockSpec(memory_space=pl.ANY)
     return pl.pallas_call(
         fused_kernel,
         out_shape=(jax.ShapeDtypeStruct((256, 128), F32), jax.ShapeDtypeStruct((1,), jnp.int32)),
-        in_specs=[smem, smem, vmem, vmem, pl.BlockSpec(memory_space=pl.ANY), vmem, vmem],
+        in_specs=[smem, smem, hbm, vmem, hbm, vmem, vmem],
         out_specs=(vmem, smem),
         scratch_shapes=[
+            pltpu.VMEM((16, 8, 2, BINS), BF16),
             pltpu.VMEM((BINS, LAGS), BF16),
             pltpu.VMEM((256, BINS), BF16),
             pltpu.VMEM((64, BINS), BF16),
@@ -351,12 +356,20 @@
             pltpu.VMEM((8, 3, 16, 128), F32),
             pltpu.VMEM((7, 256, 128), BF16),
             pltpu.VMEM((8, 256, 128), BF16),
-            sem,
+            sem, sem,
             sem((15,)), sem((15,)), sem, sem, sem((3,)), sem((3,)), sem((4, 3)), sem((4, 3)), sem((4,)), sem((4,)),
             sem((3,)), sem((3,)), sem((3,)), sem((3,)), sem, sem, sem((7,)), sem((7,)),
         ],
         compiler_params=pltpu.CompilerParams(collective_id=0, has_side_effects=True, vmem_limit_bytes=52 << 20),
     )(sources, station_rows, spectra, flags, jnp.asarray(table), jnp.asarray(turn), jnp.asarray(mirror))
+
+
+def sum_over(value, axis, size):
+    step = 1
+    while step < size:
+        value = value + lax.ppermute(value, axis, [(n, n ^ step) for n in range(size)])
+        step *= 2
+    return value
 
 
 def general(spectra, hour_flags, sources, station_rows):
@@ -369,17 +382,18 @@
     rows = station_rows[sources.reshape(-1)]
     holder, local = rows // 16, rows % 16
     mine = (holder == me)[:, None]
-    source_valid = lax.psum(jnp.where(mine, valid[local], 0.0), "sta")
+    source_valid = sum_over(jnp.where(mine, valid[local], 0.0), "sta", 32)
     shared = jnp.dot(source_valid, valid.T, precision=lax.Precision.HIGHEST)
     weights = (1.0 / jnp.maximum(shared, 1.0)).reshape(256, 1) * (1.0 / math.sqrt(BINS))
     kept = jnp.where(mine, white[:, local], 0).astype(BF16)
-    src = lax.psum(kept.reshape(256, BINS), "sta")
+    src = sum_over(kept.reshape(256, BINS), "sta", 32)
     term = correlate(white.reshape(256, BINS), src, weights).astype(F32)
-    return lax.psum_scatter(term, "day", scatter_dimension=1, tiled=True)
+    term = sum_over(term, "day", 8)
+    return lax.dynamic_slice_in_dim(term, 128 * lax.axis_index("day"), 128, 1)
 
 
 def shards(spectra, hour_flags, sources, station_rows):
-    stacked, load = fused(sources, station_rows, spectra.reshape(256, BINS), hour_flags[0])
+    stacked, load = fused(sources, station_rows, spectra[0], hour_flags[0])
     stacked = lax.cond(
         load[0] <= SLOTS,
         lambda *args: stacked,

time: 83.1 us -> 67.3 us (0.81)
  between operations: 14 us -> 0.65 us
  local copies, waits for them, and re-layouts: 4.87 us -> 1.44 us
  Pallas kernels: 63.9 us -> 64.9 us
    reshape x1 -> x0, local copies, waits for them, and re-layouts: 4.12 us -> none  [shards(): spectra.reshape(256, BINS)]
    pallas_call x1, Pallas kernels: 63.9 us -> 64.9 us  [fused(): pl.pallas_call(fused_kernel, out_shape=(jax.ShapeDtypeStruct((256, 128),...]
where the time goes in v3:
time: 67.3 us; the launch traced here: 67.2 us
  Pallas kernels  64.9 us (96%)
  local copies, waits for them, and re-layouts  1.44 us (2%)
    pallas_call x1, Pallas kernels, fused(): pl.pallas_call(fused_kernel, out_shape=(jax.ShapeDtypeStruct((256, 128),...  64.9 us

profile of v3, /device:TPU:1, one launch (start us, length us, event | category | flops | bytes accessed | tf_op | source)
XLA Modules:
  0.0 67.2 jit_solution(9924954387409580289)
XLA Ops:
  0.0 0.8 %copy.42.flags = s32[16,8]{1,0:T(8,128)S(1)} copy(s32[16,8]{0,1:T(8,128)} %bitcast.30) | data formatting | bytes 1024 | tf_op jit(solution)/shard_map/squeeze | solution.py:396
  0.8 0.0 copy-start
  0.8 0.0 copy-start.1
  0.8 0.0 copy-start.3
  0.8 0.0 copy-start.4
  0.8 0.0 copy-start.5
  0.8 0.0 copy-start.6
  0.8 64.9 %shard_map.102 = (f32[256,128]{1,0:T(8,128)S(1)}, s32[1]{0:T(128)}) custom-call(s32[2,8]{1,0:T(2,128)} %sources.1, s32[512]{0:T(512)} %rows_ref.1, bf16[16,8,2,3584]{3,2,1,0:T(2,128)(2,1)} %bitcast.26, s32[16,8]{1,0:T(8,128)S(1)} %copy.42.flags, bf16[3584,1024]{1,0:T(8,128)(2,1)} %constant.68.clone.table_hbm, f32[2,3584]{1,0:T(2,128)} %constant.69.clone.turn, ...), custom_call_target="tpu_custom_call" | custom-call | tf_op jit(solution)/shard_map/pallas_call | solution.py:338
  66.2 0.0 copy-done
  66.2 0.0 copy-done.1
  66.2 0.0 copy-done.3
  66.2 0.0 copy-done.4
  66.3 0.0 copy-done.5
  66.3 0.0 copy-done.6
  66.3 0.2 conditional.1
  66.5 0.7 copy.46
Async XLA Ops:
  0.8 65.5 %copy-start = (s32[512]{0:T(512)S(1)}, s32[512]{0:T(512)}, u32[]{:S(2)}) copy-start(s32[512]{0:T(512)} %rows_ref.1) | copy-start | bytes 6148
  0.8 65.5 %copy-start.1 = (bf16[1,16,8,2,3584]{4,3,2,1,0:T(2,128)(2,1)S(1)}, bf16[1,16,8,2,3584]{4,3,2,1,0:T(2,128)(2,1)}, u32[]{:S(2)}) copy-start(bf16[1,16,8,2,3584]{4,3,2,1,0:T(2,128)(2,1)} %param.12) | copy-start | bytes 5505028
  0.8 65.5 %copy-start.3 = (bf16[512,512]{1,0:T(8,128)(2,1)S(1)}, bf16[512,512]{1,0:T(8,128)(2,1)}, u32[]{:S(2)}) copy-start(bf16[512,512]{1,0:T(8,128)(2,1)} %constant.70.clone.mirror) | copy-start | bytes 1572868
  0.8 65.5 %copy-start.4 = (f32[2,3584]{1,0:T(2,128)S(1)}, f32[2,3584]{1,0:T(2,128)}, u32[]{:S(2)}) copy-start(f32[2,3584]{1,0:T(2,128)} %constant.69.clone.turn) | copy-start | bytes 86020
  0.8 65.5 %copy-start.5 = (s32[1,16,8]{1,2,0:T(8,128)S(1)}, s32[1,16,8]{1,2,0:T(8,128)}, u32[]{:S(2)}) copy-start(s32[1,16,8]{1,2,0:T(8,128)} %param.13) | copy-start | bytes 1540
  0.8 65.5 %copy-start.6 = (s32[2,8]{1,0:T(2,128)S(1)}, s32[2,8]{1,0:T(2,128)}, u32[]{:S(2)}) copy-start(s32[2,8]{1,0:T(2,128)} %sources.1) | copy-start | bytes 196

commit v4 on v3

--- a/solution.py
+++ b/solution.py
@@ -16,6 +16,7 @@
 QUARTER = BINS // 4
 EPSILON = 1e-06
 SLOTS = 4
+PARTS = ((0, 512), (512, 384))
 MESH = pl.DeviceIdType.MESH
 BF16 = jnp.bfloat16
 F32 = jnp.float32
@@ -150,7 +151,7 @@
         squares = values * values
         power = power + squares[:, :128] + squares[:, 128:]
     power = jnp.sum(power, axis=1, keepdims=True)
-    flag = flags[...].astype(F32)
+    flag = flags[0].astype(F32)
     for h in range(8):
         hour = 2 * (h % 4) + h // 4
         mean = (power[32 * h:32 * h + 16] + power[32 * h + 16:32 * h + 32]) * (1.0 / (2 * BINS))
@@ -184,18 +185,25 @@
     slots[...] = jnp.dot(pick, white[...], preferred_element_type=F32).astype(BF16)
     pl.semaphore_wait(barrier, 23)
 
-    copies = []
-    for n, (dz, dx) in enumerate(offsets):
-        z_to, x_to = (z + dz) % 4, (x + dx) % 4
-        copies.append(
-            remote(
-                slots.at[pl.ds(mult(16 * z_to, 16), 16), pl.ds(mult(QUARTER * x_to, 128), QUARTER)],
-                recv.at[pl.ds(mult(16 * chip, 16), 16)],
-                s_sc.at[n],
-                r_sc.at[n],
-                dev(z_to, x_to, c),
+    def lanes_of(x_of, part):
+        start, width = PARTS[part]
+        return pl.ds(mult(QUARTER * x_of + start, 128), width)
+
+    scattered = []
+    for part, (start, width) in enumerate(PARTS):
+        copies = []
+        for n, (dz, dx) in enumerate(offsets):
+            z_to, x_to = (z + dz) % 4, (x + dx) % 4
+            copies.append(
+                remote(
+                    slots.at[pl.ds(mult(16 * z_to, 16), 16), lanes_of(x_to, part)],
+                    recv.at[pl.ds(mult(16 * chip, 16), 16), pl.ds(start, width)],
+                    s_sc.at[part, n],
+                    r_sc.at[part, n],
+                    dev(z_to, x_to, c),
+                )
             )
-        )
+        scattered.append(copies)
     ref = valid.at[own_flags]
     flag_z = [remote(ref, ref, s_fz.at[n], r_fz.at[n], dev((z + 1 + n) % 4, x, c)) for n in range(3)]
     recv[pl.ds(mult(16 * chip, 16), 16), :] = slots[
@@ -220,48 +228,68 @@
     lax.fori_loop(0, BINS // 128, receiver_planes, 0)
     total[...] = jnp.zeros_like(total)
 
-    for copy in flag_z:
-        copy.wait()
-    ref = valid.at[pl.ds(mult(256 * c + 64 * x, 64), 64)]
-    flag_x = [remote(ref, ref, s_fx.at[n], r_fx.at[n], dev(z, (x + 1 + n) % 4, c)) for n in range(3)]
-    for copy in copies:
-        copy.wait()
-    picked[...] = jnp.dot(pick, recv[...], preferred_element_type=F32).astype(BF16)
-    copy = remote(picked.at[pl.ds(mult(32 * (1 - c), 32), 32)], twin, s_tw, r_tw, dev(z, x, 1 - c))
-    copy.wait()
-
-    def piece(z_of, x_of):
-        return src.at[pl.ds(mult(128 * c + 32 * z_of, 32), 32), pl.ds(mult(QUARTER * x_of, 128), QUARTER)]
-
-    def half(x_of):
-        return src.at[pl.ds(mult(128 * c, 128), 128), pl.ds(mult(QUARTER * x_of, 128), QUARTER)]
+    def piece(z_of, x_of, part):
+        return src.at[pl.ds(mult(128 * c + 32 * z_of, 32), 32), lanes_of(x_of, part)]
 
     def send(ref, s_sem, r_sem, device):
         return remote(ref, ref, s_sem, r_sem, device)
 
-    piece(z, x)[...] = picked[pl.ds(mult(32 * c, 32), 32), :] + twin[...]
-
-    def send_x(k, z_of):
+    def send_x(part, k, z_of):
+        ref = piece(z_of, x, part)
         return [
-            send(piece(z_of, x), s_x.at[k, n], r_x.at[k, n], dev(z, (x + dx) % 4, c))
+            send(ref, s_x.at[part, k, n], r_x.at[part, k, n], dev(z, (x + dx) % 4, c))
             for n, dx in enumerate((2, 1, 3))
         ]
 
-    along_z = [send(piece(z, x), s_z.at[n], r_z.at[n], dev((z + dz) % 4, x, c)) for n, dz in enumerate((2, 1, 3))]
-    along_x = [send_x(0, z)]
+    def send_across(part, n, x_of):
+        ref = src.at[pl.ds(mult(128 * c, 128), 128), lanes_of(x_of, part)]
+        return send(ref, s_t.at[part, n], r_t.at[part, n], dev(z, x, 1 - c))
+
+    along_z, along_x, across = [], [], []
+    for part, (start, width) in enumerate(PARTS):
+        for copy in scattered[part]:
+            copy.wait()
+        here = pl.ds(start, width)
+        picked[:, here] = jnp.dot(pick, recv[:, here], preferred_element_type=F32).astype(BF16)
+        copy = remote(
+            picked.at[pl.ds(mult(32 * (1 - c), 32), 32), here],
+            twin.at[:, here],
+            s_tw.at[part],
+            r_tw.at[part],
+            dev(z, x, 1 - c),
+        )
+        if part == 0:
+            for other in flag_z:
+                other.wait()
+            ref = valid.at[pl.ds(mult(256 * c + 64 * x, 64), 64)]
+            flag_x = [remote(ref, ref, s_fx.at[n], r_fx.at[n], dev(z, (x + 1 + n) % 4, c)) for n in range(3)]
+        copy.wait()
+        ref = piece(z, x, part)
+        ref[...] = picked[pl.ds(mult(32 * c, 32), 32), here] + twin[:, here]
+        along_z.append(
+            [
+                send(ref, s_z.at[part, n], r_z.at[part, n], dev((z + dz) % 4, x, c))
+                for n, dz in enumerate((2, 1, 3))
+            ]
+        )
+        along_x.append([send_x(part, 0, z)])
+    for part in range(len(PARTS)):
+        for n, dz in ((1, 1), (2, 3), (0, 2)):
+            along_z[part][n].wait()
+            along_x[part].append(send_x(part, 1 + n, (z + 4 - dz) % 4))
+        across.append([send_across(part, 0, x)])
     for copy in flag_x:
         copy.wait()
     ref = valid.at[pl.ds(mult(256 * c, 256), 256)]
     flag_t = remote(ref, ref, s_ft, r_ft, dev(z, x, 1 - c))
-    for n, dz in ((1, 1), (2, 3), (0, 2)):
-        along_z[n].wait()
-        along_x.append(send_x(1 + n, (z + 4 - dz) % 4))
-
-    def correlate_quarter(q):
+
+    def correlate_part(q, part):
+        start, width = PARTS[part]
+
         def tile(t, carry):
-            all_lanes = pl.ds(mult(QUARTER * q + 128 * t, 128), 128)
+            all_lanes = pl.ds(mult(QUARTER * q + start + 128 * t, 128), 128)
             lanes = pl.ds(mult(128 * t, 128), 128)
-            at = 7 * q + t
+            at = 7 * q + start // 128 + t
             co, si = turn[0:1, all_lanes], turn[1:2, all_lanes]
             for h in range(8):
                 a = src[pl.ds(32 * h, 16), all_lanes].astype(F32)
@@ -283,12 +311,24 @@
                     cross[1, rows, lanes] = (sums[n][0] - sums[n][2]).astype(BF16)
             return carry
 
-        lax.fori_loop(0, 7, tile, 0)
-        bins = pl.ds(mult(QUARTER * q, 128), QUARTER)
-        total[0] += jnp.dot(cross[0], table[bins, 0:HALF], preferred_element_type=F32)
-        total[1] += jnp.dot(cross[1], table[bins, HALF:], preferred_element_type=F32)
-
-    across = [send(half(x), s_t.at[0], r_t.at[0], dev(z, x, 1 - c))]
+        lax.fori_loop(0, width // 128, tile, 0)
+        bins = lanes_of(q, part)
+        total[0] += jnp.dot(cross[0, :, 0:width], table[bins, 0:HALF], preferred_element_type=F32)
+        total[1] += jnp.dot(cross[1, :, 0:width], table[bins, HALF:], preferred_element_type=F32)
+
+    def take_x(part, n, dx):
+        for k in range(4):
+            along_x[part][k][n].wait()
+        across[part].append(send_across(part, 1 + n, (x + 4 - dx) % 4))
+
+    table_copy.wait()
+    across[0][0].wait()
+    correlate_part(x, 0)
+    for n, dx in ((1, 1), (2, 3)):
+        take_x(0, n, dx)
+    across[1][0].wait()
+    correlate_part(x, 1)
+    take_x(0, 0, 2)
     flag_t.wait()
     ri = lax.broadcasted_iota(jnp.int32, (256, 512), 0)
     ci = lax.broadcasted_iota(jnp.int32, (256, 512), 1)
@@ -301,15 +341,21 @@
     shared = jnp.sum(shared, axis=1, keepdims=True)
     scale = (1.0 / jnp.maximum(shared, 1.0)) * (1.0 / math.sqrt(BINS))
 
-    table_copy.wait()
-    across[0].wait()
-    correlate_quarter(x)
-    for n, dx in ((1, 1), (2, 3), (0, 2)):
-        for k in range(4):
-            along_x[k][n].wait()
-        copy = send(half((x + 4 - dx) % 4), s_t.at[1 + n], r_t.at[1 + n], dev(z, x, 1 - c))
-        copy.wait()
-        correlate_quarter((x + 4 - dx) % 4)
+    across[0][1].wait()
+    correlate_part((x + 3) % 4, 0)
+    for n, dx in ((1, 1), (2, 3)):
+        take_x(1, n, dx)
+    across[0][2].wait()
+    correlate_part((x + 1) % 4, 0)
+    take_x(1, 0, 2)
+    across[0][3].wait()
+    correlate_part((x + 2) % 4, 0)
+    across[1][1].wait()
+    correlate_part((x + 3) % 4, 1)
+    across[1][2].wait()
+    correlate_part((x + 1) % 4, 1)
+    across[1][3].wait()
+    correlate_part((x + 2) % 4, 1)
 
     even, odd = total[0] * scale, total[1] * scale
     for n in range(4):
@@ -357,7 +403,8 @@
             pltpu.VMEM((7, 256, 128), BF16),
             pltpu.VMEM((8, 256, 128), BF16),
             sem, sem,
-            sem((15,)), sem((15,)), sem, sem, sem((3,)), sem((3,)), sem((4, 3)), sem((4, 3)), sem((4,)), sem((4,)),
+            sem((2, 15)), sem((2, 15)), sem((2,)), sem((2,)), sem((2, 3)), sem((2, 3)), sem((2, 4, 3)), sem((2, 4, 3)),
+            sem((2, 4)), sem((2, 4)),
             sem((3,)), sem((3,)), sem((3,)), sem((3,)), sem, sem, sem((7,)), sem((7,)),
         ],
         compiler_params=pltpu.CompilerParams(collective_id=0, has_side_effects=True, vmem_limit_bytes=52 << 20),
@@ -393,7 +440,7 @@
 
 
 def shards(spectra, hour_flags, sources, station_rows):
-    stacked, load = fused(sources, station_rows, spectra[0], hour_flags[0])
+    stacked, load = fused(sources, station_rows, spectra[0], hour_flags)
     stacked = lax.cond(
         load[0] <= SLOTS,
         lambda *args: stacked,

time: 67.3 us -> 59.6 us (0.89)
  Pallas kernels: 64.9 us -> 57.1 us
    pallas_call x1, Pallas kernels: 64.9 us -> 57.1 us  [fused(): pl.pallas_call(fused_kernel, out_shape=(jax.ShapeDtypeStruct((256, 128),...]
    unnamed x13 -> x14, local copies, waits for them, and re-layouts: 0.69 us -> 1.44 us
    squeeze x1 -> x0, local copies, waits for them, and re-layouts: 0.76 us -> none  [shards(): stacked, load = fused(sources, station_rows, spectra[0], hour_flags[0])]
where the time goes in v4:
time: 59.6 us; the launch traced here: 59.5 us
  Pallas kernels  57.1 us (96%)
  local copies, waits for them, and re-layouts  1.44 us (2%)
  between operations  0.65 us (1%)
    pallas_call x1, Pallas kernels, fused(): pl.pallas_call(fused_kernel, out_shape=(jax.ShapeDtypeStruct((256, 128),...  57.1 us
    unnamed x14, local copies, waits for them, and re-layouts  1.44 us

profile of v4, /device:TPU:1, one launch (start us, length us, event | category | flops | bytes accessed | tf_op | source)
XLA Modules:
  0.0 59.5 jit_solution(7319746858599588396)
XLA Ops:
  0.0 0.8 %copy.42.flags = s32[1,16,8]{2,1,0:T(8,128)S(1)} copy(s32[1,16,8]{1,2,0:T(8,128)} %param.13) | data formatting | bytes 1024 | tf_op args[1]
  0.8 0.0 copy-start
  0.8 0.0 copy-start.1
  0.8 0.0 copy-start.3
  0.8 0.0 copy-start.4
  0.8 0.0 copy-start.5
  0.8 0.0 copy-start.6
  0.8 57.1 %shard_map.102 = (f32[256,128]{1,0:T(8,128)S(1)}, s32[1]{0:T(128)}) custom-call(s32[2,8]{1,0:T(2,128)} %sources.1, s32[512]{0:T(512)} %rows_ref.1, bf16[16,8,2,3584]{3,2,1,0:T(2,128)(2,1)} %bitcast.25, s32[1,16,8]{2,1,0:T(8,128)S(1)} %copy.42.flags, bf16[3584,1024]{1,0:T(8,128)(2,1)} %constant.68.clone.table_hbm, f32[2,3584]{1,0:T(2,128)} %constant.69.clone.turn, ...), custom_call_target="tpu_custom_call" | custom-call | tf_op jit(solution)/shard_map/pallas_call | solution.py:384
  58.5 0.0 copy-done
  58.5 0.0 copy-done.1
  58.5 0.0 copy-done.3
  58.5 0.0 copy-done.4
  58.5 0.0 copy-done.5
  58.5 0.0 copy-done.6
  58.6 0.2 conditional.1
  58.8 0.7 %copy.46 = f32[16,16,128]{2,1,0:T(8,128)} copy(f32[16,16,128]{2,1,0:T(8,128)S(1)} %get-tuple-element.36) | data formatting | bytes 262144
Async XLA Ops:
  0.8 57.7 %copy-start = (s32[512]{0:T(512)S(1)}, s32[512]{0:T(512)}, u32[]{:S(2)}) copy-start(s32[512]{0:T(512)} %rows_ref.1) | copy-start | bytes 6148
  0.8 57.7 %copy-start.1 = (bf16[1,16,8,2,3584]{4,3,2,1,0:T(2,128)(2,1)S(1)}, bf16[1,16,8,2,3584]{4,3,2,1,0:T(2,128)(2,1)}, u32[]{:S(2)}) copy-start(bf16[1,16,8,2,3584]{4,3,2,1,0:T(2,128)(2,1)} %param.12) | copy-start | bytes 5505028
  0.8 57.8 %copy-start.3 = (bf16[512,512]{1,0:T(8,128)(2,1)S(1)}, bf16[512,512]{1,0:T(8,128)(2,1)}, u32[]{:S(2)}) copy-start(bf16[512,512]{1,0:T(8,128)(2,1)} %constant.70.clone.mirror) | copy-start | bytes 1572868
  0.8 57.8 %copy-start.4 = (f32[2,3584]{1,0:T(2,128)S(1)}, f32[2,3584]{1,0:T(2,128)}, u32[]{:S(2)}) copy-start(f32[2,3584]{1,0:T(2,128)} %constant.69.clone.turn) | copy-start | bytes 86020
  0.8 57.8 %copy-start.5 = (s32[1,16,8]{1,2,0:T(8,128)S(1)}, s32[1,16,8]{1,2,0:T(8,128)}, u32[]{:S(2)}) copy-start(s32[1,16,8]{1,2,0:T(8,128)} %param.13) | copy-start | bytes 1540
  0.8 57.8 %copy-start.6 = (s32[2,8]{1,0:T(2,128)S(1)}, s32[2,8]{1,0:T(2,128)}, u32[]{:S(2)}) copy-start(s32[2,8]{1,0:T(2,128)} %sources.1) | copy-start | bytes 196

commit v5 on v4

--- a/solution.py
+++ b/solution.py
@@ -16,7 +16,7 @@
 QUARTER = BINS // 4
 EPSILON = 1e-06
 SLOTS = 4
-PARTS = ((0, 512), (512, 384))
+PARTS = ((0, 384), (384, 512))
 MESH = pl.DeviceIdType.MESH
 BF16 = jnp.bfloat16
 F32 = jnp.float32
@@ -110,7 +110,7 @@
 
 
 def fused_kernel(sources, rows_ref, spectra_hbm, flags, table_hbm, turn, mirror, out, load, spectra, table, white, slots, recv, picked,
-                 twin, src, valid, cross, total, rec_f, src_f, days, daily, s_spec, s_tab, s_sc, r_sc, s_tw, r_tw, s_z, r_z,
+                 twin, src, valid, cross, total, rec_f, src_f, scale_ref, days, daily, s_spec, s_tab, s_sc, r_sc, s_tw, r_tw, s_z, r_z,
                  s_x, r_x, s_t, r_t, s_fz, r_fz, s_fx, r_fx, s_ft, r_ft, s_d, r_d):
     day = lax.axis_index("day")
     me = lax.axis_index("sta")
@@ -273,62 +273,58 @@
             ]
         )
         along_x.append([send_x(part, 0, z)])
-    for part in range(len(PARTS)):
-        for n, dz in ((1, 1), (2, 3), (0, 2)):
-            along_z[part][n].wait()
-            along_x[part].append(send_x(part, 1 + n, (z + 4 - dz) % 4))
-        across.append([send_across(part, 0, x)])
-    for copy in flag_x:
-        copy.wait()
-    ref = valid.at[pl.ds(mult(256 * c, 256), 256)]
-    flag_t = remote(ref, ref, s_ft, r_ft, dev(z, x, 1 - c))
-
-    def correlate_part(q, part):
+    def products(q, part, into, blocks, keep, fresh):
         start, width = PARTS[part]
 
         def tile(t, carry):
             all_lanes = pl.ds(mult(QUARTER * q + start + 128 * t, 128), 128)
             lanes = pl.ds(mult(128 * t, 128), 128)
             at = 7 * q + start // 128 + t
-            co, si = turn[0:1, all_lanes], turn[1:2, all_lanes]
-            for h in range(8):
-                a = src[pl.ds(32 * h, 16), all_lanes].astype(F32)
-                b = src[pl.ds(32 * h + 16, 16), all_lanes].astype(F32)
-                a_turn, b_turn = a * co + b * si, b * co - a * si
-                src_f[h, 0], src_f[h, 1], src_f[h, 2] = a_turn + b_turn, b_turn, a_turn
-            for block in range(4):
+            if fresh:
+                co, si = turn[0:1, all_lanes], turn[1:2, all_lanes]
+                for h in range(8):
+                    a = src[pl.ds(32 * h, 16), all_lanes].astype(F32)
+                    b = src[pl.ds(32 * h + 16, 16), all_lanes].astype(F32)
+                    a_turn, b_turn = a * co + b * si, b * co - a * si
+                    src_f[keep + t, h, 0] = a_turn + b_turn
+                    src_f[keep + t, h, 1] = b_turn
+                    src_f[keep + t, h, 2] = a_turn
+            for block in blocks:
                 sums = [[None] * 3 for _ in range(4)]
                 for h in range(8):
                     rec = [rec_f[at, h, k] for k in range(3)]
                     for n in range(4):
                         for k in range(3):
-                            row = src_f[h, k, pl.ds(block * 4 + n, 1), :]
+                            row = src_f[keep + t, h, k, pl.ds(block * 4 + n, 1), :]
                             term = jnp.broadcast_to(row, (16, 128)) * rec[k]
                             sums[n][k] = term if h == 0 else sums[n][k] + term
                 for n in range(4):
                     rows = pl.ds(16 * (block * 4 + n), 16)
-                    cross[0, rows, lanes] = (sums[n][0] - sums[n][1]).astype(BF16)
-                    cross[1, rows, lanes] = (sums[n][0] - sums[n][2]).astype(BF16)
+                    cross[into, 0, rows, lanes] = (sums[n][0] - sums[n][1]).astype(BF16)
+                    cross[into, 1, rows, lanes] = (sums[n][0] - sums[n][2]).astype(BF16)
             return carry
 
         lax.fori_loop(0, width // 128, tile, 0)
+
+    def to_lags(q, part, into, rows):
+        start, width = PARTS[part]
         bins = lanes_of(q, part)
-        total[0] += jnp.dot(cross[0, :, 0:width], table[bins, 0:HALF], preferred_element_type=F32)
-        total[1] += jnp.dot(cross[1, :, 0:width], table[bins, HALF:], preferred_element_type=F32)
+        total[0, rows] += jnp.dot(cross[into, 0, rows, 0:width], table[bins, 0:HALF], preferred_element_type=F32)
+        total[1, rows] += jnp.dot(cross[into, 1, rows, 0:width], table[bins, HALF:], preferred_element_type=F32)
+
+    def correlate_part(q, part):
+        products(q, part, 0, range(4), 0, True)
+        to_lags(q, part, 0, pl.ds(0, 256))
 
     def take_x(part, n, dx):
         for k in range(4):
             along_x[part][k][n].wait()
         across[part].append(send_across(part, 1 + n, (x + 4 - dx) % 4))
 
-    table_copy.wait()
-    across[0][0].wait()
-    correlate_part(x, 0)
-    for n, dx in ((1, 1), (2, 3)):
-        take_x(0, n, dx)
-    across[1][0].wait()
-    correlate_part(x, 1)
-    take_x(0, 0, 2)
+    for copy in flag_x:
+        copy.wait()
+    ref = valid.at[pl.ds(mult(256 * c, 256), 256)]
+    flag_t = remote(ref, ref, s_ft, r_ft, dev(z, x, 1 - c))
     flag_t.wait()
     ri = lax.broadcasted_iota(jnp.int32, (256, 512), 0)
     ci = lax.broadcasted_iota(jnp.int32, (256, 512), 1)
@@ -339,34 +335,58 @@
     choose = jnp.where(ci == target, 1.0, 0.0).astype(BF16)
     shared = jnp.dot(choose, valid[...], preferred_element_type=F32) * jnp.concatenate([wide] * 16, axis=0)
     shared = jnp.sum(shared, axis=1, keepdims=True)
-    scale = (1.0 / jnp.maximum(shared, 1.0)) * (1.0 / math.sqrt(BINS))
-
+    scale_ref[...] = (1.0 / jnp.maximum(shared, 1.0)) * (1.0 / math.sqrt(BINS))
+
+    def take_z(part):
+        for n, dz in ((1, 1), (2, 3), (0, 2)):
+            along_z[part][n].wait()
+            along_x[part].append(send_x(part, 1 + n, (z + 4 - dz) % 4))
+        across.append([send_across(part, 0, x)])
+
+    table_copy.wait()
+    take_z(0)
+    across[0][0].wait()
+    correlate_part(x, 0)
+    take_z(1)
+    for n, dx in ((1, 1), (2, 3)):
+        take_x(0, n, dx)
+    across[1][0].wait()
+    correlate_part(x, 1)
+    take_x(0, 0, 2)
     across[0][1].wait()
     correlate_part((x + 3) % 4, 0)
-    for n, dx in ((1, 1), (2, 3)):
-        take_x(1, n, dx)
     across[0][2].wait()
     correlate_part((x + 1) % 4, 0)
-    take_x(1, 0, 2)
     across[0][3].wait()
     correlate_part((x + 2) % 4, 0)
-    across[1][1].wait()
-    correlate_part((x + 3) % 4, 1)
-    across[1][2].wait()
-    correlate_part((x + 1) % 4, 1)
-    across[1][3].wait()
-    correlate_part((x + 2) % 4, 1)
-
-    even, odd = total[0] * scale, total[1] * scale
-    for n in range(4):
-        daily[4 + n] = (even - odd)[:, 128 * n:128 * n + 128].astype(BF16)
-    back = jnp.dot((even + odd).astype(BF16), mirror[...], preferred_element_type=F32)
-    for n in range(4):
-        daily[n] = back[:, 128 * n:128 * n + 128].astype(BF16)
+    for n, dx in ((1, 1), (2, 3), (0, 2)):
+        take_x(1, n, dx)
     copies = []
-    for n in (4, 3, 5, 2, 6, 1, 7):
-        to = (day + n) % 8
-        copies.append(remote(daily.at[to], days.at[n - 1], s_d.at[n - 1], r_d.at[n - 1], (to, me)))
+    for half in range(2):
+        rows = pl.ds(128 * half, 128)
+        for n, dx in enumerate((3, 1, 2)):
+            if half == 0:
+                across[1][1 + n].wait()
+            products((x + dx) % 4, 1, n, range(2 * half, 2 * half + 2), 4 * n, half == 0)
+        for n, dx in enumerate((3, 1, 2)):
+            to_lags((x + dx) % 4, 1, n, rows)
+        even, odd = total[0, rows] * scale_ref[rows, :], total[1, rows] * scale_ref[rows, :]
+        for n in range(4):
+            daily[4 + n, rows] = (even - odd)[:, 128 * n:128 * n + 128].astype(BF16)
+        back = jnp.dot((even + odd).astype(BF16), mirror[...], preferred_element_type=F32)
+        for n in range(4):
+            daily[n, rows] = back[:, 128 * n:128 * n + 128].astype(BF16)
+        for n in (4, 3, 5, 2, 6, 1, 7):
+            to = (day + n) % 8
+            copies.append(
+                remote(
+                    daily.at[to, rows],
+                    days.at[n - 1, rows],
+                    s_d.at[half, n - 1],
+                    r_d.at[half, n - 1],
+                    (to, me),
+                )
+            )
     for copy in copies:
         copy.wait()
     result = daily[day].astype(F32)
@@ -396,16 +416,17 @@
             pltpu.VMEM((32, QUARTER), BF16),
             pltpu.VMEM((256, BINS), BF16),
             pltpu.VMEM((512, 128), BF16),
-            pltpu.VMEM((2, 256, QUARTER), BF16),
+            pltpu.VMEM((3, 2, 256, 512), BF16),
             pltpu.VMEM((2, 256, HALF), F32),
             pltpu.VMEM((BINS // 128, 8, 3, 16, 128), F32),
-            pltpu.VMEM((8, 3, 16, 128), F32),
+            pltpu.VMEM((12, 8, 3, 16, 128), F32),
+            pltpu.VMEM((256, 1), F32),
             pltpu.VMEM((7, 256, 128), BF16),
             pltpu.VMEM((8, 256, 128), BF16),
             sem, sem,
             sem((2, 15)), sem((2, 15)), sem((2,)), sem((2,)), sem((2, 3)), sem((2, 3)), sem((2, 4, 3)), sem((2, 4, 3)),
             sem((2, 4)), sem((2, 4)),
-            sem((3,)), sem((3,)), sem((3,)), sem((3,)), sem, sem, sem((7,)), sem((7,)),
+            sem((3,)), sem((3,)), sem((3,)), sem((3,)), sem, sem, sem((2, 7)), sem((2, 7)),
         ],
         compiler_params=pltpu.CompilerParams(collective_id=0, has_side_effects=True, vmem_limit_bytes=52 << 20),
     )(sources, station_rows, spectra, flags, jnp.asarray(table), jnp.asarray(turn), jnp.asarray(mirror))

time: 59.6 us -> 57.9 us (0.971)
  Pallas kernels: 57.1 us -> 55.5 us
    pallas_call x1, Pallas kernels: 57.1 us -> 55.5 us  [fused(): pl.pallas_call(fused_kernel, out_shape=(jax.ShapeDtypeStruct((256, 128),...]
where the time goes in v5:
time: 57.9 us; the launch traced here: 57.8 us
  Pallas kernels  55.5 us (96%)
  local copies, waits for them, and re-layouts  1.44 us (2%)
  between operations  0.65 us (1%)
    pallas_call x1, Pallas kernels, fused(): pl.pallas_call(fused_kernel, out_shape=(jax.ShapeDtypeStruct((256, 128),...  55.5 us
    unnamed x14, local copies, waits for them, and re-layouts  1.44 us

profile of v5, /device:TPU:1, one launch (start us, length us, event | category | flops | bytes accessed | tf_op | source)
XLA Modules:
  0.0 57.8 jit_solution(5682793239925581799)
XLA Ops:
  0.0 0.8 %copy.42.flags = s32[1,16,8]{2,1,0:T(8,128)S(1)} copy(s32[1,16,8]{1,2,0:T(8,128)} %param.13) | data formatting | bytes 1024 | tf_op args[1]
  0.8 0.0 copy-start
  0.8 0.0 copy-start.1
  0.8 0.0 copy-start.3
  0.8 0.0 copy-start.4
  0.8 0.0 copy-start.5
  0.8 0.0 copy-start.6
  0.8 55.5 %shard_map.102 = (f32[256,128]{1,0:T(8,128)S(1)}, s32[1]{0:T(128)}) custom-call(s32[2,8]{1,0:T(2,128)} %sources.1, s32[512]{0:T(512)} %rows_ref.1, bf16[16,8,2,3584]{3,2,1,0:T(2,128)(2,1)} %bitcast.25, s32[1,16,8]{2,1,0:T(8,128)S(1)} %copy.42.flags, bf16[3584,1024]{1,0:T(8,128)(2,1)} %constant.68.clone.table_hbm, f32[2,3584]{1,0:T(2,128)} %constant.69.clone.turn, ...), custom_call_target="tpu_custom_call" | custom-call | tf_op jit(solution)/shard_map/pallas_call | solution.py:404
  56.8 0.0 copy-done
  56.8 0.0 copy-done.1
  56.8 0.0 copy-done.3
  56.9 0.0 copy-done.4
  56.9 0.0 copy-done.5
  56.9 0.0 copy-done.6
  56.9 0.2 conditional.1
  57.1 0.7 %copy.46 = f32[16,16,128]{2,1,0:T(8,128)} copy(f32[16,16,128]{2,1,0:T(8,128)S(1)} %get-tuple-element.36) | data formatting | bytes 262144
Async XLA Ops:
  0.8 56.1 %copy-start = (s32[512]{0:T(512)S(1)}, s32[512]{0:T(512)}, u32[]{:S(2)}) copy-start(s32[512]{0:T(512)} %rows_ref.1) | copy-start | bytes 6148
  0.8 56.1 %copy-start.1 = (bf16[1,16,8,2,3584]{4,3,2,1,0:T(2,128)(2,1)S(1)}, bf16[1,16,8,2,3584]{4,3,2,1,0:T(2,128)(2,1)}, u32[]{:S(2)}) copy-start(bf16[1,16,8,2,3584]{4,3,2,1,0:T(2,128)(2,1)} %param.12) | copy-start | bytes 5505028
  0.8 56.1 %copy-start.3 = (bf16[512,512]{1,0:T(8,128)(2,1)S(1)}, bf16[512,512]{1,0:T(8,128)(2,1)}, u32[]{:S(2)}) copy-start(bf16[512,512]{1,0:T(8,128)(2,1)} %constant.70.clone.mirror) | copy-start | bytes 1572868
  0.8 56.1 %copy-start.4 = (f32[2,3584]{1,0:T(2,128)S(1)}, f32[2,3584]{1,0:T(2,128)}, u32[]{:S(2)}) copy-start(f32[2,3584]{1,0:T(2,128)} %constant.69.clone.turn) | copy-start | bytes 86020
  0.8 56.1 %copy-start.5 = (s32[1,16,8]{1,2,0:T(8,128)S(1)}, s32[1,16,8]{1,2,0:T(8,128)}, u32[]{:S(2)}) copy-start(s32[1,16,8]{1,2,0:T(8,128)} %param.13) | copy-start | bytes 1540
  0.8 56.1 %copy-start.6 = (s32[2,8]{1,0:T(2,128)S(1)}, s32[2,8]{1,0:T(2,128)}, u32[]{:S(2)}) copy-start(s32[2,8]{1,0:T(2,128)} %sources.1) | copy-start | bytes 196

commit v6 on v5

--- a/solution.py
+++ b/solution.py
@@ -357,10 +357,11 @@
     correlate_part((x + 3) % 4, 0)
     across[0][2].wait()
     correlate_part((x + 1) % 4, 0)
+    for n, dx in ((1, 1), (2, 3)):
+        take_x(1, n, dx)
     across[0][3].wait()
     correlate_part((x + 2) % 4, 0)
-    for n, dx in ((1, 1), (2, 3), (0, 2)):
-        take_x(1, n, dx)
+    take_x(1, 0, 2)
     copies = []
     for half in range(2):
         rows = pl.ds(128 * half, 128)

time: 57.9 us -> 57 us (0.984)
  Pallas kernels: 55.5 us -> 54.6 us
    pallas_call x1, Pallas kernels: 55.5 us -> 54.6 us  [fused(): pl.pallas_call(fused_kernel, out_shape=(jax.ShapeDtypeStruct((256, 128),...]
where the time goes in v6:
time: 57 us; the launch traced here: 56.9 us
  Pallas kernels  54.6 us (96%)
  local copies, waits for them, and re-layouts  1.44 us (3%)
  between operations  0.65 us (1%)
    pallas_call x1, Pallas kernels, fused(): pl.pallas_call(fused_kernel, out_shape=(jax.ShapeDtypeStruct((256, 128),...  54.6 us
    unnamed x14, local copies, waits for them, and re-layouts  1.44 us

profile of v6, /device:TPU:1, one launch (start us, length us, event | category | flops | bytes accessed | tf_op | source)
XLA Modules:
  0.0 56.9 jit_solution(7270325742117122473)
XLA Ops:
  0.0 0.8 %copy.42.flags = s32[1,16,8]{2,1,0:T(8,128)S(1)} copy(s32[1,16,8]{1,2,0:T(8,128)} %param.13) | data formatting | bytes 1024 | tf_op args[1]
  0.8 0.0 copy-start
  0.8 0.0 copy-start.1
  0.8 0.0 copy-start.3
  0.8 0.0 copy-start.4
  0.8 0.0 copy-start.5
  0.8 0.0 copy-start.6
  0.8 54.6 %shard_map.102 = (f32[256,128]{1,0:T(8,128)S(1)}, s32[1]{0:T(128)}) custom-call(s32[2,8]{1,0:T(2,128)} %sources.1, s32[512]{0:T(512)} %rows_ref.1, bf16[16,8,2,3584]{3,2,1,0:T(2,128)(2,1)} %bitcast.25, s32[1,16,8]{2,1,0:T(8,128)S(1)} %copy.42.flags, bf16[3584,1024]{1,0:T(8,128)(2,1)} %constant.68.clone.table_hbm, f32[2,3584]{1,0:T(2,128)} %constant.69.clone.turn, ...), custom_call_target="tpu_custom_call" | custom-call | tf_op jit(solution)/shard_map/pallas_call | solution.py:405
  55.9 0.0 copy-done
  56.0 0.0 copy-done.1
  56.0 0.0 copy-done.3
  56.0 0.0 copy-done.4
  56.0 0.0 copy-done.5
  56.0 0.0 copy-done.6
  56.0 0.2 conditional.1
  56.2 0.7 %copy.46 = f32[16,16,128]{2,1,0:T(8,128)} copy(f32[16,16,128]{2,1,0:T(8,128)S(1)} %get-tuple-element.36) | data formatting | bytes 262144
Async XLA Ops:
  0.8 55.2 %copy-start = (s32[512]{0:T(512)S(1)}, s32[512]{0:T(512)}, u32[]{:S(2)}) copy-start(s32[512]{0:T(512)} %rows_ref.1) | copy-start | bytes 6148
  0.8 55.2 %copy-start.1 = (bf16[1,16,8,2,3584]{4,3,2,1,0:T(2,128)(2,1)S(1)}, bf16[1,16,8,2,3584]{4,3,2,1,0:T(2,128)(2,1)}, u32[]{:S(2)}) copy-start(bf16[1,16,8,2,3584]{4,3,2,1,0:T(2,128)(2,1)} %param.12) | copy-start | bytes 5505028
  0.8 55.2 %copy-start.3 = (bf16[512,512]{1,0:T(8,128)(2,1)S(1)}, bf16[512,512]{1,0:T(8,128)(2,1)}, u32[]{:S(2)}) copy-start(bf16[512,512]{1,0:T(8,128)(2,1)} %constant.70.clone.mirror) | copy-start | bytes 1572868
  0.8 55.2 %copy-start.4 = (f32[2,3584]{1,0:T(2,128)S(1)}, f32[2,3584]{1,0:T(2,128)}, u32[]{:S(2)}) copy-start(f32[2,3584]{1,0:T(2,128)} %constant.69.clone.turn) | copy-start | bytes 86020
  0.8 55.2 %copy-start.5 = (s32[1,16,8]{1,2,0:T(8,128)S(1)}, s32[1,16,8]{1,2,0:T(8,128)}, u32[]{:S(2)}) copy-start(s32[1,16,8]{1,2,0:T(8,128)} %param.13) | copy-start | bytes 1540
  0.8 55.2 %copy-start.6 = (s32[2,8]{1,0:T(2,128)S(1)}, s32[2,8]{1,0:T(2,128)}, u32[]{:S(2)}) copy-start(s32[2,8]{1,0:T(2,128)} %sources.1) | copy-start | bytes 196
